TPU v7x, 32 devices: a whole 2x2x4 slice. The times are simulated.
32 devices in a mesh: dp: 8 (over z, y), seq: 4 (over x, core).
Axes of the slice: x: 2, y: 2, z: 4, core: 2. Of those that a mesh axis runs over, the one named last changes fastest.
Arguments:
- frames: bfloat16 [8, 1536, 1024], P('dp', 'seq'), may hold values from -6 to 6
- output_gradient: bfloat16 [8, 1536, 1024], P('dp', 'seq'), may hold values from -6 to 6
- segment_lengths: int32 [8, 4], P('dp'), may hold values from 1 to 1533, as said below
- time_index: int32 [8, 4], P('dp'), may hold values from 0 to 999
- query_weight: bfloat16 [1024, 1024], P(('dp', 'seq')), may hold values from -0.1875 to 0.1875
- query_bias: bfloat16 [1024], P(('dp', 'seq')), may hold values from -3 to 3
- key_weight: bfloat16 [1024, 1024], P(('dp', 'seq')), may hold values from -0.1875 to 0.1875
- key_bias: bfloat16 [1024], P(('dp', 'seq')), may hold values from -3 to 3
- value_weight: bfloat16 [1024, 1024], P(('dp', 'seq')), may hold values from -0.1875 to 0.1875
- value_bias: bfloat16 [1024], P(('dp', 'seq')), may hold values from -3 to 3
- output_projection: bfloat16 [1024, 1024], P(('dp', 'seq')), may hold values from -2.5 to 2.5
- output_bias: bfloat16 [1024], P(('dp', 'seq')), may hold values from -3 to 3
- up_weight: bfloat16 [1024, 2048], P(('dp', 'seq')), may hold values from -0.1875 to 0.1875
- up_bias: bfloat16 [2048], P(('dp', 'seq')), may hold values from -3 to 3
- down_weight: bfloat16 [2048, 1024], P(('dp', 'seq')), may hold values from -0.125 to 0.125
- down_bias: bfloat16 [1024], P(('dp', 'seq')), may hold values from -3 to 3
- modulation_weight: bfloat16 [1024, 6144], P(('dp', 'seq')), may hold values from -0.1875 to 0.1875
- modulation_bias: bfloat16 [6144], P(('dp', 'seq')), may hold values from -3 to 3
Outputs:
- layer_output: bfloat16 [8, 1536, 1024], P('dp', 'seq')
- frames_grad: bfloat16 [8, 1536, 1024], P('dp', 'seq')
- query_weight_grad: float32 [1024, 1024], P(('dp', 'seq'))
- query_bias_grad: float32 [1024], P(('dp', 'seq'))
- key_weight_grad: float32 [1024, 1024], P(('dp', 'seq'))
- key_bias_grad: float32 [1024], P(('dp', 'seq'))
- value_weight_grad: float32 [1024, 1024], P(('dp', 'seq'))
- value_bias_grad: float32 [1024], P(('dp', 'seq'))
- output_weight_grad: float32 [1024, 1024], P(('dp', 'seq'))
- output_bias_grad: float32 [1024], P(('dp', 'seq'))
- up_weight_grad: float32 [1024, 2048], P(('dp', 'seq'))
- up_bias_grad: float32 [2048], P(('dp', 'seq'))
- down_weight_grad: float32 [2048, 1024], P(('dp', 'seq'))
- down_bias_grad: float32 [1024], P(('dp', 'seq'))
- modulation_weight_grad: float32 [1024, 6144], P(('dp', 'seq'))
- modulation_bias_grad: float32 [6144], P(('dp', 'seq'))
Inputs may be any that keep to these rules, and one draw needn't show every extreme that they name: `segment_lengths`: in each packed row the 4 lengths sum to 1536; one utterance is longer than 1152, the others shorter than 96; in one row of every draw the others have a single frame each.
All inputs are finite; a program needn't handle non-finite values.
Results may differ from a plain program's by a relative error of at most 0.035.
Values may be sent and summed in bfloat16 or wider, within the bound.
A program may use at most 192 MiB of HBM per device.

v0:
```python
from functools import partial
import math

import jax
import jax.numpy as jnp
from jax import lax
from jax.sharding import PartitionSpec as P

HEAD_DIM = 64
MODEL_WIDTH = 1024
SEGS = 4


EPSILON = 1e-06
NEGATIVE = -1e30
HIGHEST = lax.Precision.HIGHEST


def modulated_norm(values, shift_part, scale_part):
    center = jnp.mean(values, axis=-1, keepdims=True)
    centered = values - center
    variance = jnp.mean(centered * centered, axis=-1, keepdims=True)
    return centered * lax.rsqrt(variance + EPSILON) * (1.0 + scale_part) + shift_part


def rotate(values, cosines, sines_table):
    shaped = values.reshape(values.shape[:-1] + (values.shape[-1] // HEAD_DIM, HEAD_DIM))
    first_half = shaped[..., : HEAD_DIM // 2]
    second_half = shaped[..., HEAD_DIM // 2 :]
    cosine = cosines[..., None, :]
    sine_part = sines_table[..., None, :]
    turned = jnp.concatenate(
        [
            first_half * cosine - second_half * sine_part,
            second_half * cosine + first_half * sine_part,
        ],
        axis=-1,
    )
    return turned.reshape(values.shape)


def gelu_tanh(values):
    return jax.nn.gelu(values, approximate=True)


def time_features(time_index):
    halfway = MODEL_WIDTH // 2
    frequency = jnp.exp(jnp.arange(halfway, dtype=jnp.float32) * (-math.log(10000.0) / halfway))
    angles = time_index.astype(jnp.float32)[..., None] * frequency
    return jnp.concatenate([jnp.sin(angles), jnp.cos(angles)], axis=-1)


def segment_starts(segment_lengths):
    return jnp.cumsum(segment_lengths, axis=1) - segment_lengths


def segment_numbers(segment_lengths, frame_positions):
    starts = segment_starts(segment_lengths)
    inside = (frame_positions[None, :, None] >= starts[:, None, :]).astype(jnp.int32)
    return jnp.sum(inside, axis=2) - 1


def segment_layout(segment_lengths, frame_positions):
    starts = segment_starts(segment_lengths)
    segment = segment_numbers(segment_lengths, frame_positions)
    onehot = (segment[..., None] == jnp.arange(SEGS, dtype=jnp.int32)).astype(jnp.float32)
    offset = jnp.sum(onehot * starts[:, None, :].astype(jnp.float32), axis=2)
    relative = frame_positions[None, :].astype(jnp.float32) - offset
    return (onehot, relative)


def rope_tables(relative):
    halfway = HEAD_DIM // 2
    frequency = jnp.exp(jnp.arange(halfway, dtype=jnp.float32) * (-math.log(10000.0) / halfway))
    angles = relative[..., None] * frequency
    return (jnp.cos(angles), jnp.sin(angles))


def project(values, matrix, offset):
    return jnp.einsum(
        "rld,de->rle", values, matrix, preferred_element_type=jnp.float32
    ) + offset.astype(jnp.float32)


def project_back(gradient, matrix):
    return jnp.einsum("rle,de->rld", gradient, matrix, preferred_element_type=jnp.float32)


def weight_gradient(values, gradient):
    return jnp.einsum("rld,rle->de", values, gradient, preferred_element_type=jnp.float32)


def bias_gradient(gradient):
    return jnp.sum(gradient.astype(jnp.float32), axis=(0, 1))


def lift_up(member):
    return member.reshape((1, 1) + member.shape)


def settle(member):
    return member.reshape((-1,) + member.shape[3:])


def spread(member, wide_count, narrow_count):
    return member.reshape((wide_count, narrow_count, -1) + member.shape[1:])


def unpack(member):
    return member.reshape(member.shape[2:])


def on_device(
    frames,
    output_gradient,
    segment_lengths,
    time_index,
    query_weight,
    query_bias,
    key_weight,
    key_bias,
    value_weight,
    value_bias,
    output_projection,
    output_bias,
    up_weight,
    up_bias,
    down_weight,
    down_bias,
    modulation_weight,
    modulation_bias,
):
    narrow_count = lax.axis_size("seq")
    wide_count = lax.axis_size("dp")
    seq_index = lax.axis_index("seq")
    row_count, span_frames, width_total = frames.shape
    row_length = span_frames * narrow_count
    block_rows = min(512, row_length)
    block_count = row_length // block_rows
    local_weights = (
        query_weight,
        query_bias,
        key_weight,
        key_bias,
        value_weight,
        value_bias,
        output_projection,
        output_bias,
        up_weight,
        up_bias,
        down_weight,
        down_bias,
        modulation_bias,
    )
    lifted = [lift_up(member) for member in local_weights]
    halfway_set = (
        lax.all_gather(lifted[0], "dp", axis=0, tiled=True),
        lax.all_gather(lifted[1], "dp", axis=0, tiled=True),
        lax.all_gather(lifted[2], "dp", axis=0, tiled=True),
        lax.all_gather(lifted[3], "dp", axis=0, tiled=True),
        lax.all_gather(lifted[4], "dp", axis=0, tiled=True),
        lax.all_gather(lifted[5], "dp", axis=0, tiled=True),
        lax.all_gather(lifted[6], "dp", axis=0, tiled=True),
        lax.all_gather(lifted[7], "dp", axis=0, tiled=True),
        lax.all_gather(lifted[8], "dp", axis=0, tiled=True),
        lax.all_gather(lifted[9], "dp", axis=0, tiled=True),
        lax.all_gather(lifted[10], "dp", axis=0, tiled=True),
        lax.all_gather(lifted[11], "dp", axis=0, tiled=True),
        lax.all_gather(lifted[12], "dp", axis=0, tiled=True),
    )
    complete_set = (
        lax.all_gather(halfway_set[0], "seq", axis=1, tiled=True),
        lax.all_gather(halfway_set[1], "seq", axis=1, tiled=True),
        lax.all_gather(halfway_set[2], "seq", axis=1, tiled=True),
        lax.all_gather(halfway_set[3], "seq", axis=1, tiled=True),
        lax.all_gather(halfway_set[4], "seq", axis=1, tiled=True),
        lax.all_gather(halfway_set[5], "seq", axis=1, tiled=True),
        lax.all_gather(halfway_set[6], "seq", axis=1, tiled=True),
        lax.all_gather(halfway_set[7], "seq", axis=1, tiled=True),
        lax.all_gather(halfway_set[8], "seq", axis=1, tiled=True),
        lax.all_gather(halfway_set[9], "seq", axis=1, tiled=True),
        lax.all_gather(halfway_set[10], "seq", axis=1, tiled=True),
        lax.all_gather(halfway_set[11], "seq", axis=1, tiled=True),
        lax.all_gather(halfway_set[12], "seq", axis=1, tiled=True),
    )
    gathered = [settle(member) for member in complete_set]
    (
        full_query,
        full_query_bias,
        full_key,
        full_key_bias,
        full_value,
        full_value_bias,
        full_output,
        full_output_bias,
        full_up,
        full_up_bias,
        full_down,
        full_down_bias,
        full_modulation_bias,
    ) = gathered
    local_positions = seq_index * span_frames + jnp.arange(span_frames, dtype=jnp.int32)
    local_onehot, local_relative = segment_layout(segment_lengths, local_positions)
    row_segment = segment_numbers(segment_lengths, jnp.arange(row_length, dtype=jnp.int32))
    cosines, sines_table = rope_tables(local_relative)
    turning = partial(rotate, cosines=cosines, sines_table=sines_table)
    owned_rows = modulation_weight.shape[0]
    owned_start = (lax.axis_index("dp") * narrow_count + seq_index) * owned_rows
    every_time = lax.all_gather(time_index, "dp", axis=0, tiled=True)
    every_low = jax.nn.silu(time_features(every_time)).astype(jnp.bfloat16)
    owned_low = lax.dynamic_slice_in_dim(every_low, owned_start, owned_rows, 2)
    partial_modulation = jnp.einsum(
        "rsd,dc->rsc", owned_low, modulation_weight, preferred_element_type=jnp.float32
    )
    row_share = lax.psum_scatter(partial_modulation, "dp", scatter_dimension=0, tiled=True)
    modulation = lax.psum(row_share.astype(jnp.bfloat16), "seq").astype(
        jnp.float32
    ) + full_modulation_bias.astype(jnp.float32)
    per_frame = jnp.einsum("rls,rsc->rlc", local_onehot, modulation, precision=HIGHEST)
    shift_one, scale_one, gate_one, shift_two, scale_two, gate_two = jnp.split(
        per_frame, 6, axis=-1
    )
    inputs = frames.astype(jnp.float32)
    normed, norm_back = jax.vjp(modulated_norm, inputs, shift_one, scale_one)
    normed_low = normed.astype(jnp.bfloat16)
    query_pre = project(normed_low, full_query, full_query_bias)
    key_pre = project(normed_low, full_key, full_key_bias)
    value_low = project(normed_low, full_value, full_value_bias).astype(jnp.bfloat16)
    query_turned, query_back = jax.vjp(turning, query_pre)
    key_turned, key_back = jax.vjp(turning, key_pre)
    query_heads, key_heads, value_heads = (
        lax.all_to_all(
            query_turned.astype(jnp.bfloat16), "seq", split_axis=2, concat_axis=1, tiled=True
        ),
        lax.all_to_all(
            key_turned.astype(jnp.bfloat16), "seq", split_axis=2, concat_axis=1, tiled=True
        ),
        lax.all_to_all(value_low, "seq", split_axis=2, concat_axis=1, tiled=True),
    )
    local_heads = query_heads.shape[2] // HEAD_DIM
    head_shape = (row_count, row_length, local_heads, HEAD_DIM)
    queries = query_heads.reshape(head_shape)
    keys_all = key_heads.reshape(head_shape)
    values_all = value_heads.reshape(head_shape)
    scaling = HEAD_DIM ** (-0.5)
    positions_all = jnp.arange(row_count * block_count, dtype=jnp.int32)

    def fetch_block(position):
        row_index = position // block_count
        start_row = position % block_count * block_rows
        key_row = lax.dynamic_index_in_dim(keys_all, row_index, 0, keepdims=False)
        value_row = lax.dynamic_index_in_dim(values_all, row_index, 0, keepdims=False)
        segment_row = lax.dynamic_index_in_dim(row_segment, row_index, 0, keepdims=False)
        query_block = lax.dynamic_slice_in_dim(
            lax.dynamic_index_in_dim(queries, row_index, 0, keepdims=False),
            start_row,
            block_rows,
            0,
        )
        segment_block = lax.dynamic_slice_in_dim(segment_row, start_row, block_rows, 0)
        scores = (
            jnp.einsum("bhd,khd->hbk", query_block, key_row, preferred_element_type=jnp.float32)
            * scaling
        )
        scores = jnp.where((segment_block[:, None] == segment_row[None, :])[None], scores, NEGATIVE)
        return (row_index, start_row, query_block, key_row, value_row, scores)

    def forward_block(position):
        row_index, start_row, query_block, key_row, value_row, scores = fetch_block(position)
        highest = jnp.max(scores, axis=2, keepdims=True)
        weights = jnp.exp(scores - highest)
        totals = jnp.sum(weights, axis=2, keepdims=True)
        probabilities = (weights / totals).astype(jnp.bfloat16)
        mixed_block = jnp.einsum(
            "hbk,khd->bhd", probabilities, value_row, preferred_element_type=jnp.float32
        )
        return (
            mixed_block.astype(jnp.bfloat16).reshape(block_rows, -1),
            (highest + jnp.log(totals))[..., 0],
        )

    mixed_blocks, logsums = lax.map(forward_block, positions_all)
    attention_heads = mixed_blocks.reshape(row_count, row_length, -1)
    attention_frames = lax.all_to_all(
        attention_heads, "seq", split_axis=1, concat_axis=2, tiled=True
    )
    branch = project(attention_frames, full_output, full_output_bias)
    middle = inputs + gate_one * branch
    normed_two, norm_two_back = jax.vjp(modulated_norm, middle, shift_two, scale_two)
    normed_two_low = normed_two.astype(jnp.bfloat16)
    hidden = project(normed_two_low, full_up, full_up_bias)
    activated, gelu_back = jax.vjp(gelu_tanh, hidden)
    activated_low = activated.astype(jnp.bfloat16)
    branch_two = project(activated_low, full_down, full_down_bias)
    layer_output = (middle + gate_two * branch_two).astype(jnp.bfloat16)
    cotangent = output_gradient.astype(jnp.float32)
    grad_branch_two = (gate_two * cotangent).astype(jnp.bfloat16)
    grad_gate_two = cotangent * branch_two
    grad_activated = project_back(grad_branch_two, full_down)
    grad_hidden = gelu_back(grad_activated)[0].astype(jnp.bfloat16)
    grad_normed_two = project_back(grad_hidden, full_up)
    grad_middle_part, grad_shift_two, grad_scale_two = norm_two_back(grad_normed_two)
    grad_middle = cotangent + grad_middle_part
    grad_gate_one = grad_middle * branch
    grad_branch = (gate_one * grad_middle).astype(jnp.bfloat16)
    grad_attention = project_back(grad_branch, full_output).astype(jnp.bfloat16)
    grad_heads = lax.all_to_all(grad_attention, "seq", split_axis=2, concat_axis=1, tiled=True)
    grad_outputs = grad_heads.reshape(head_shape)

    def backward_block(running, pair_inputs):
        grad_keys, grad_values = running
        position, logsum = pair_inputs
        row_index, start_row, query_block, key_row, value_row, scores = fetch_block(position)
        grad_block = lax.dynamic_slice_in_dim(
            lax.dynamic_index_in_dim(grad_outputs, row_index, 0, keepdims=False),
            start_row,
            block_rows,
            0,
        )
        probabilities = jnp.exp(scores - logsum[..., None])
        grad_probabilities = jnp.einsum(
            "bhd,khd->hbk", grad_block, value_row, preferred_element_type=jnp.float32
        )
        delta_sum = jnp.sum(probabilities * grad_probabilities, axis=2, keepdims=True)
        grad_scores = (probabilities * (grad_probabilities - delta_sum)).astype(jnp.bfloat16)
        grad_query_block = (
            jnp.einsum("hbk,khd->bhd", grad_scores, key_row, preferred_element_type=jnp.float32)
            * scaling
        )
        key_part = (
            jnp.einsum("hbk,bhd->khd", grad_scores, query_block, preferred_element_type=jnp.float32)
            * scaling
        )
        value_part = jnp.einsum(
            "hbk,bhd->khd",
            probabilities.astype(jnp.bfloat16),
            grad_block,
            preferred_element_type=jnp.float32,
        )
        grad_keys = lax.dynamic_update_index_in_dim(
            grad_keys,
            lax.dynamic_index_in_dim(grad_keys, row_index, 0, keepdims=False) + key_part,
            row_index,
            0,
        )
        grad_values = lax.dynamic_update_index_in_dim(
            grad_values,
            lax.dynamic_index_in_dim(grad_values, row_index, 0, keepdims=False) + value_part,
            row_index,
            0,
        )
        return (
            (grad_keys, grad_values),
            grad_query_block.astype(jnp.bfloat16).reshape(block_rows, -1),
        )

    zero_heads = jnp.zeros(head_shape, jnp.float32)
    (grad_keys_all, grad_values_all), grad_query_blocks = lax.scan(
        backward_block, (zero_heads, zero_heads), (positions_all, logsums)
    )
    flat_shape = (row_count, row_length, -1)
    grad_query_frames, grad_key_frames, grad_value_frames = (
        lax.all_to_all(
            grad_query_blocks.reshape(flat_shape), "seq", split_axis=1, concat_axis=2, tiled=True
        ),
        lax.all_to_all(
            grad_keys_all.reshape(flat_shape).astype(jnp.bfloat16),
            "seq",
            split_axis=1,
            concat_axis=2,
            tiled=True,
        ),
        lax.all_to_all(
            grad_values_all.reshape(flat_shape).astype(jnp.bfloat16),
            "seq",
            split_axis=1,
            concat_axis=2,
            tiled=True,
        ),
    )
    grad_query_pre = query_back(grad_query_frames.astype(jnp.float32))[0].astype(jnp.bfloat16)
    grad_key_pre = key_back(grad_key_frames.astype(jnp.float32))[0].astype(jnp.bfloat16)
    grad_normed = (
        project_back(grad_query_pre, full_query)
        + project_back(grad_key_pre, full_key)
        + project_back(grad_value_frames, full_value)
    )
    grad_inputs_part, grad_shift_one, grad_scale_one = norm_back(grad_normed)
    frames_grad = (grad_middle + grad_inputs_part).astype(jnp.bfloat16)
    grad_per_frame = jnp.concatenate(
        [
            grad_shift_one,
            grad_scale_one,
            grad_gate_one,
            grad_shift_two,
            grad_scale_two,
            grad_gate_two,
        ],
        axis=-1,
    )
    grad_modulation = jnp.einsum("rls,rlc->rsc", local_onehot, grad_per_frame, precision=HIGHEST)
    gradients = (
        weight_gradient(normed_low, grad_query_pre),
        bias_gradient(grad_query_pre),
        weight_gradient(normed_low, grad_key_pre),
        bias_gradient(grad_key_pre),
        weight_gradient(normed_low, grad_value_frames),
        bias_gradient(grad_value_frames),
        weight_gradient(attention_frames, grad_branch),
        bias_gradient(grad_branch),
        weight_gradient(normed_two_low, grad_hidden),
        bias_gradient(grad_hidden),
        weight_gradient(activated_low, grad_branch_two),
        bias_gradient(grad_branch_two),
        jnp.sum(grad_modulation, axis=(0, 1)),
    )
    row_total = lax.psum(grad_modulation.astype(jnp.bfloat16), "seq").astype(jnp.float32)
    every_grad = lax.all_gather(row_total.astype(jnp.bfloat16), "dp", axis=0, tiled=True).astype(
        row_total.dtype
    )
    modulation_weight_grad = jnp.einsum(
        "rsd,rsc->dc", owned_low.astype(jnp.float32), every_grad, precision=HIGHEST
    )
    spreaded = [spread(member, wide_count, narrow_count) for member in gradients]
    first_pass = (
        lax.psum_scatter(
            spreaded[0].astype(jnp.bfloat16), "seq", scatter_dimension=1, tiled=True
        ).astype(jnp.float32),
        lax.psum_scatter(
            spreaded[1].astype(jnp.bfloat16), "seq", scatter_dimension=1, tiled=True
        ).astype(jnp.float32),
        lax.psum_scatter(
            spreaded[2].astype(jnp.bfloat16), "seq", scatter_dimension=1, tiled=True
        ).astype(jnp.float32),
        lax.psum_scatter(
            spreaded[3].astype(jnp.bfloat16), "seq", scatter_dimension=1, tiled=True
        ).astype(jnp.float32),
        lax.psum_scatter(
            spreaded[4].astype(jnp.bfloat16), "seq", scatter_dimension=1, tiled=True
        ).astype(jnp.float32),
        lax.psum_scatter(
            spreaded[5].astype(jnp.bfloat16), "seq", scatter_dimension=1, tiled=True
        ).astype(jnp.float32),
        lax.psum_scatter(
            spreaded[6].astype(jnp.bfloat16), "seq", scatter_dimension=1, tiled=True
        ).astype(jnp.float32),
        lax.psum_scatter(
            spreaded[7].astype(jnp.bfloat16), "seq", scatter_dimension=1, tiled=True
        ).astype(jnp.float32),
        lax.psum_scatter(
            spreaded[8].astype(jnp.bfloat16), "seq", scatter_dimension=1, tiled=True
        ).astype(jnp.float32),
        lax.psum_scatter(
            spreaded[9].astype(jnp.bfloat16), "seq", scatter_dimension=1, tiled=True
        ).astype(jnp.float32),
        lax.psum_scatter(
            spreaded[10].astype(jnp.bfloat16), "seq", scatter_dimension=1, tiled=True
        ).astype(jnp.float32),
        lax.psum_scatter(
            spreaded[11].astype(jnp.bfloat16), "seq", scatter_dimension=1, tiled=True
        ).astype(jnp.float32),
        lax.psum_scatter(
            spreaded[12].astype(jnp.bfloat16), "seq", scatter_dimension=1, tiled=True
        ).astype(jnp.float32),
    )
    second_pass = (
        lax.psum_scatter(first_pass[0], "dp", scatter_dimension=0, tiled=True),
        lax.psum_scatter(first_pass[1], "dp", scatter_dimension=0, tiled=True),
        lax.psum_scatter(first_pass[2], "dp", scatter_dimension=0, tiled=True),
        lax.psum_scatter(first_pass[3], "dp", scatter_dimension=0, tiled=True),
        lax.psum_scatter(first_pass[4], "dp", scatter_dimension=0, tiled=True),
        lax.psum_scatter(first_pass[5], "dp", scatter_dimension=0, tiled=True),
        lax.psum_scatter(first_pass[6], "dp", scatter_dimension=0, tiled=True),
        lax.psum_scatter(first_pass[7], "dp", scatter_dimension=0, tiled=True),
        lax.psum_scatter(first_pass[8], "dp", scatter_dimension=0, tiled=True),
        lax.psum_scatter(first_pass[9], "dp", scatter_dimension=0, tiled=True),
        lax.psum_scatter(first_pass[10], "dp", scatter_dimension=0, tiled=True),
        lax.psum_scatter(first_pass[11], "dp", scatter_dimension=0, tiled=True),
        lax.psum_scatter(first_pass[12], "dp", scatter_dimension=0, tiled=True),
    )
    reduced = [unpack(member) for member in second_pass]
    return (
        layer_output,
        frames_grad,
        reduced[0],
        reduced[1],
        reduced[2],
        reduced[3],
        reduced[4],
        reduced[5],
        reduced[6],
        reduced[7],
        reduced[8],
        reduced[9],
        reduced[10],
        reduced[11],
        modulation_weight_grad,
        reduced[12],
    )


def solution(mesh):
    return jax.shard_map(
        on_device,
        mesh=mesh,
        in_specs=(
            P("dp", "seq", None),
            P("dp", "seq", None),
            P("dp", None),
            P("dp", None),
            P(("dp", "seq"), None),
            P(("dp", "seq")),
            P(("dp", "seq"), None),
            P(("dp", "seq")),
            P(("dp", "seq"), None),
            P(("dp", "seq")),
            P(("dp", "seq"), None),
            P(("dp", "seq")),
            P(("dp", "seq"), None),
            P(("dp", "seq")),
            P(("dp", "seq"), None),
            P(("dp", "seq")),
            P(("dp", "seq"), None),
            P(("dp", "seq")),
        ),
        out_specs=(
            P("dp", "seq", None),
            P("dp", "seq", None),
            P(("dp", "seq"), None),
            P(("dp", "seq")),
            P(("dp", "seq"), None),
            P(("dp", "seq")),
            P(("dp", "seq"), None),
            P(("dp", "seq")),
            P(("dp", "seq"), None),
            P(("dp", "seq")),
            P(("dp", "seq"), None),
            P(("dp", "seq")),
            P(("dp", "seq"), None),
            P(("dp", "seq")),
            P(("dp", "seq"), None),
            P(("dp", "seq")),
        ),
        check_vma=False,
    )
```

profile of v0, /device:TPU:0, one launch (start us, length us, event | category | flops | bytes accessed | tf_op | source)
XLA Modules:
  0.0 1468.2 jit_solution(5612676406868496026)
XLA Ops:
  8.0 35.7 %all-gather.1 = bf16[256,1024]{1,0:T(8,128)(2,1)} all-gather(bf16[32,1024]{1,0:T(8,128)(2,1)} %param.26), channel_id=3, replica_groups=mesh['dp'=8,'seq'=4] {'dp'}, dimensions={0}, use_global_device_ids=true | all-gather | bytes 589824 | tf_op jit(solution)/shard_map/all_gather | solution.py:157
  43.7 34.3 %all-gather.3 = bf16[256,1024]{1,0:T(8,128)(2,1)} all-gather(bf16[32,1024]{1,0:T(8,128)(2,1)} %param.28), channel_id=5, replica_groups=mesh['dp'=8,'seq'=4] {'dp'}, dimensions={0}, use_global_device_ids=true | all-gather | bytes 589824 | tf_op jit(solution)/shard_map/all_gather | solution.py:159
  78.2 33.5 %all-gather.5 = bf16[256,1024]{1,0:T(8,128)(2,1)} all-gather(bf16[32,1024]{1,0:T(8,128)(2,1)S(1)} %copy-done.54), channel_id=7, replica_groups=mesh['dp'=8,'seq'=4] {'dp'}, dimensions={0}, use_global_device_ids=true | all-gather | bytes 589824 | tf_op jit(solution)/shard_map/all_gather | solution.py:161
  112.3 33.3 %all-gather.7 = bf16[256,1024]{1,0:T(8,128)(2,1)} all-gather(bf16[32,1024]{1,0:T(8,128)(2,1)S(1)} %copy-done.55), channel_id=9, replica_groups=mesh['dp'=8,'seq'=4] {'dp'}, dimensions={0}, use_global_device_ids=true | all-gather | bytes 589824 | tf_op jit(solution)/shard_map/all_gather | solution.py:163
  145.8 20.4 %all-gather.13 = s32[8,1,4]{2,1,0:T(1,128)S(1)} all-gather(s32[1,1,4]{2,1,0:T(1,128)S(1)} %bitcast.501), channel_id=1, replica_groups=mesh['dp'=8,'seq'=4] {'dp'}, dimensions={0}, use_global_device_ids=true | all-gather | bytes 144 | tf_op jit(solution)/shard_map/all_gather | solution.py:209
  167.7 41.5 %all-reduce.39 = bf16[8,4,6144]{2,1,0:T(4,128)(2,1)S(1)} all-reduce(f32[8,4,6144]{2,1,0:T(4,128)S(1)} %fusion.98), channel_id=15, replica_groups=mesh['dp'=8,'seq'=4] {'dp'}, use_global_device_ids=true, to_apply=%region_2.3.clone | all-reduce | flops 196608 | bytes 1179648
  213.6 20.0 %all-reduce.32 = (bf16[1536]{0:T(1024)(128)(2,1)S(1)}, bf16[256]{0:T(256)(128)(2,1)S(1)}, bf16[256]{0:T(256)(128)(2,1)S(1)}, bf16[256]{0:T(256)(128)(2,1)S(1)}, ...) all-reduce(bf16[1536]{0:T(1024)(128)(2,1)S(1)} %dynamic-update-slic, ...), channel_id=2, replica_groups=mesh['dp'=8,'seq'=4] {'dp'}, use_global_device_ids=true, to_apply=%add.4 | all-reduce | flops 3328 | bytes 13312
  250.5 11.7 psum.14
  312.6 12.5 all_gather.98
  363.0 39.8 %while.30 = (s32[]{:T(128)}, bf16[3,512,256]{2,1,0:T(8,128)(2,1)}, f32[3,4,512]{2,1,0:T(4,128)S(1)}, s32[3]{0:T(128)S(1)}, s32[1,1536]{1,0:T(1,128)S(1)}, /*inde...) while((s32[]{:T(128)}, bf16[3,512,256]{2,1,0:T(8,128)(2,1)}, ...), condition=%wide.region_11.12_spmd, body=%wide.region_8.11_spmd.sunk | while | flops 843970560 | bytes 44131080 | solution.py:282
  406.7 10.0 reduce.29
  423.1 12.5 all_gather.102
  510.7 11.6 all-to-all-done.4
  532.7 115.8 %while.31 = (s32[]{:T(128)}, f32[1,1536,4,64]{1,3,2,0:T(8,128)}, f32[1,1536,4,64]{1,3,2,0:T(8,128)}, bf16[3,512,256]{2,1,0:T(8,128)(2,1)}, s32[3]{0:T(128)S(1)},...) while((s32[]{:T(128)}, f32[1,1536,4,64]{1,3,2,0:T(8,128)}, ...), condition=%wide.region_18.19_spmd, body=%wide.region_16.18_spmd.sunk | while | flops 2043803648 | bytes 232850480 | solution.py:358
  669.2 8.8 copy.409
  762.7 266.9 %all-reduce.38.cloned.1.call-done = (bf16[8,4,32,1024]{3,2,1,0:T(8,128)(2,1)}, bf16[8,4,32,1024]{3,2,1,0:T(8,128)(2,1)}, bf16[8,4,32,1024]{3,2,1,0:T(8,128)(2,1)...) async-done(((bf16[8,4,32,1024]{3,2,1,0:T(8,128)(2,1)}, bf16[8,4,32,1024]{3,2,1,0:T(8,128)(2,1)}, ...) | async-done | bytes 16777232
  1048.8 11.2 all-reduce.33
  1064.0 31.8 %all_gather.111 = bf16[8,4,6144]{2,1,0:T(4,128)(2,1)S(1)} all-gather(bf16[1,4,6144]{2,1,0:T(4,128)(2,1)S(1)} %get-tuple-element.322), channel_id=1, replica_groups=mesh['dp'=8,'seq'=4] {'dp'}, dimensions={0}, use_global_device_ids=true | all-gather | bytes 442368 | tf_op jit(solution)/shard_map/all_gather | solution.py:418
  1097.7 37.1 %all-reduce.31 = (f32[8,1,32]{2,1,0:T(1,128)S(1)}, f32[8,1,32]{2,1,0:T(1,128)S(1)}, f32[8,1,32]{2,1,0:T(1,128)S(1)}, f32[8,1,32]{2,1,0:T(1,128)S(1)}, f32[8,1,64...) all-reduce(f32[8,1,32]{2,1,0:T(1,128)S(1)} %bitcast.499, ...), channel_id=19, replica_groups=mesh['dp'=8,'seq'=4] {'dp'}, use_global_device_ids=true, to_apply=%region_25.26.clone | all-reduce | flops 3328 | bytes 26624
  1140.6 45.2 %reduce-scatter.30.cloned.1.call-done = f32[1,1,32,1024]{3,2,1,0:T(8,128)} async-done(((f32[8,1,32,1024]{3,2,1,0:T(8,128)}), f32[1,1,32,1024]{3,2,1,0:T(8,128)}) %reduce-scatter.30.cloned.1.call-update) | async-done | bytes 131088 | tf_op jit(solution)/shard_map/reduce_scatter | solution.py:471
  1185.8 66.9 %reduce-scatter.32.cloned.1.call-done = f32[1,1,32,1024]{3,2,1,0:T(8,128)} async-done(((f32[8,1,32,1024]{3,2,1,0:T(8,128)}), f32[1,1,32,1024]{3,2,1,0:T(8,128)}) %reduce-scatter.32.cloned.1.call-update) | async-done | bytes 131088 | tf_op jit(solution)/shard_map/reduce_scatter | solution.py:473
  1252.7 66.4 %reduce-scatter.26.cloned.1.call-done = f32[1,1,32,1024]{3,2,1,0:T(8,128)} async-done(((f32[8,1,32,1024]{3,2,1,0:T(8,128)}), f32[1,1,32,1024]{3,2,1,0:T(8,128)}) %reduce-scatter.26.cloned.1.call-update) | async-done | bytes 131088 | tf_op jit(solution)/shard_map/reduce_scatter | solution.py:467
  1319.1 71.2 %reduce-scatter.34.cloned.1.call-done = f32[1,1,32,2048]{3,2,1,0:T(8,128)} async-done(((f32[8,1,32,2048]{3,2,1,0:T(8,128)}), f32[1,1,32,2048]{3,2,1,0:T(8,128)}) %reduce-scatter.34.cloned.1.call-update) | async-done | bytes 262160 | tf_op jit(solution)/shard_map/reduce_scatter | solution.py:475
  1390.3 71.1 %reduce-scatter.36.cloned.1.call-done = f32[1,1,64,1024]{3,2,1,0:T(8,128)} async-done(((f32[8,1,64,1024]{3,2,1,0:T(8,128)}), f32[1,1,64,1024]{3,2,1,0:T(8,128)}) %reduce-scatter.36.cloned.1.call-update) | async-done | bytes 262160 | tf_op jit(solution)/shard_map/reduce_scatter | solution.py:477
  (565 shorter events, 492.4 us)
Async XLA Ops:
  7.2 160.4 %all-gather.35.cloned.1.call-start = ((), (), s32[]{:S(2)}) async-start(), calls=%async_computation.28 | async-start | bytes 1179648 | tf_op jit(solution)/shard_map/all_gather | solution.py:165
  8.0 262.9 %all-gather.23.cloned.1.call-start = ((), (), s32[]{:S(2)}) async-start(), calls=%async_computation.15 | async-start | bytes 2621440 | tf_op jit(solution)/shard_map/all_gather | solution.py:172
  43.7 233.1 %all-gather.25.cloned.1.call-start = ((), (), s32[]{:S(2)}) async-start(), calls=%async_computation.16 | async-start | bytes 2621440 | tf_op jit(solution)/shard_map/all_gather | solution.py:174
  78.1 247.1 %all-gather.27.cloned.1.call-start = ((), (), s32[]{:S(2)}) async-start(), calls=%async_computation.17 | async-start | bytes 2621440 | tf_op jit(solution)/shard_map/all_gather | solution.py:176
  111.7 229.1 %all-gather.37.cloned.1.call-start = ((), (), s32[]{:S(2)}) async-start(), calls=%async_computation.29 | async-start | bytes 1179648 | tf_op jit(solution)/shard_map/all_gather | solution.py:167
  112.3 346.3 %all-gather.29.cloned.1.call-start = ((), (), s32[]{:S(2)}) async-start(), calls=%async_computation.18 | async-start | bytes 2621440 | tf_op jit(solution)/shard_map/all_gather | solution.py:178
  145.8 320.8 %all-gather.31.cloned.1.call-start = ((), (), s32[]{:S(2)}) async-start(), calls=%async_computation.19 | async-start | bytes 5242880 | tf_op jit(solution)/shard_map/all_gather | solution.py:180
  293.1 15.1 %all-to-all-start.1 = ((bf16[4,2,49152]{2,1,0:T(2,128)(2,1)}), bf16[4,2,49152]{2,1,0:T(2,128)(2,1)S(1)}, u32[]{:S(2)}, u32[]{:S(2)}) async-start(bf16[4,2,49152]{2,1,0:T(2,128)(2,1)} %reshape.1199), calls=%async_computation.1 | async-start | bytes 1572864 | tf_op jit(solution)/shard_map/all_to_all | solution.py:235
  308.3 28.1 %all-to-all-start = ((bf16[4,2,49152]{2,1,0:T(2,128)(2,1)}), bf16[4,2,49152]{2,1,0:T(2,128)(2,1)}, u32[]{:S(2)}, u32[]{:S(2)}) async-start(bf16[4,2,49152]{2,1,0:T(2,128)(2,1)} %reshape.1197), calls=%async_computation | async-start | bytes 1572864 | tf_op jit(solution)/shard_map/all_to_all | solution.py:232
  336.4 17.2 %all-to-all-start.2 = ((bf16[4,2,49152]{2,1,0:T(2,128)(2,1)}), bf16[4,2,49152]{2,1,0:T(2,128)(2,1)}, u32[]{:S(2)}, u32[]{:S(2)}) async-start(bf16[4,2,49152]{2,1,0:T(2,128)(2,1)} %reshape.1201), calls=%async_computation.2 | async-start | bytes 1572864 | tf_op jit(solution)/shard_map/all_to_all | solution.py:238
  340.6 133.0 %all-gather.33.cloned.1.call-start = ((), (), s32[]{:S(2)}) async-start(), calls=%async_computation.20 | async-start | bytes 5242880 | tf_op jit(solution)/shard_map/all_gather | solution.py:182
  418.7 30.9 %all-to-all-start.3 = ((bf16[4,2,49152]{2,1,0:T(2,128)(2,1)}), bf16[4,2,49152]{2,1,0:T(2,128)(2,1)}, u32[]{:S(2)}, u32[]{:S(2)}) async-start(bf16[4,2,49152]{2,1,0:T(2,128)(2,1)} %reshape.1203), calls=%async_computation.3 | async-start | bytes 1572864 | tf_op jit(solution)/shard_map/all_to_all | solution.py:284
  507.2 15.1 %all-to-all-start.4 = ((bf16[4,2,49152]{2,1,0:T(2,128)(2,1)}), bf16[4,2,49152]{2,1,0:T(2,128)(2,1)S(1)}, u32[]{:S(2)}, u32[]{:S(2)}) async-start(bf16[4,2,49152]{2,1,0:T(2,128)(2,1)} %reshape.1205), calls=%async_computation.4 | async-start | bytes 1572864 | tf_op jit(solution)/shard_map/all_to_all | solution.py:307
  660.8 26.3 %all-to-all-start.6 = ((bf16[4,2,49152]{2,1,0:T(2,128)(2,1)}), bf16[4,2,49152]{2,1,0:T(2,128)(2,1)S(1)}, u32[]{:S(2)}, u32[]{:S(2)}) async-start(bf16[4,2,49152]{2,1,0:T(2,128)(2,1)} %reshape.1209), calls=%async_computation.6 | async-start | bytes 1572864 | tf_op jit(solution)/shard_map/all_to_all | solution.py:366
  687.1 24.9 %all-to-all-start.5 = ((bf16[4,2,49152]{2,1,0:T(2,128)(2,1)}), bf16[4,2,49152]{2,1,0:T(2,128)(2,1)}, u32[]{:S(2)}, u32[]{:S(2)}) async-start(bf16[4,2,49152]{2,1,0:T(2,128)(2,1)} %reshape.1207), calls=%async_computation.5 | async-start | bytes 1572864 | tf_op jit(solution)/shard_map/all_to_all | solution.py:363
  712.0 15.9 %all-to-all-start.7 = ((bf16[4,2,49152]{2,1,0:T(2,128)(2,1)}), bf16[4,2,49152]{2,1,0:T(2,128)(2,1)}, u32[]{:S(2)}, u32[]{:S(2)}) async-start(bf16[4,2,49152]{2,1,0:T(2,128)(2,1)} %reshape.1211), calls=%async_computation.7 | async-start | bytes 1572864 | tf_op jit(solution)/shard_map/all_to_all | solution.py:373
  716.3 313.3 %all-reduce.38.cloned.1.call-start = ((), (), s32[]{:S(2)}) async-start(), calls=%async_computation.30 | async-start | bytes 33554432
  742.3 354.7 %reduce-scatter.38.cloned.1.call-start = ((), (), s32[]{:S(2)}) async-start(), calls=%async_computation.27 | async-start | bytes 20480 | tf_op jit(solution)/shard_map/reduce_scatter | solution.py:462
  762.6 377.9 %reduce-scatter.28.cloned.1.call-start = ((), (), s32[]{:S(2)}) async-start(), calls=%async_computation.22 | async-start | bytes 1179648 | tf_op jit(solution)/shard_map/reduce_scatter | solution.py:469
  1032.4 153.4 %reduce-scatter.30.cloned.1.call-start = ((), (), s32[]{:S(2)}) async-start(), calls=%async_computation.23 | async-start | bytes 1179648 | tf_op jit(solution)/shard_map/reduce_scatter | solution.py:471
  1035.3 217.4 %reduce-scatter.32.cloned.1.call-start = ((), (), s32[]{:S(2)}) async-start(), calls=%async_computation.24 | async-start | bytes 1179648 | tf_op jit(solution)/shard_map/reduce_scatter | solution.py:473
  1038.1 280.9 %reduce-scatter.26.cloned.1.call-start = ((), (), s32[]{:S(2)}) async-start(), calls=%async_computation.21 | async-start | bytes 1179648 | tf_op jit(solution)/shard_map/reduce_scatter | solution.py:467
  1041.0 349.3 %reduce-scatter.34.cloned.1.call-start = ((), (), s32[]{:S(2)}) async-start(), calls=%async_computation.25 | async-start | bytes 2359296 | tf_op jit(solution)/shard_map/reduce_scatter | solution.py:475
  1044.5 416.9 %reduce-scatter.36.cloned.1.call-start = ((), (), s32[]{:S(2)}) async-start(), calls=%async_computation.26 | async-start | bytes 2359296 | tf_op jit(solution)/shard_map/reduce_scatter | solution.py:477
  (113 other events, 2209.6 us)
Sparse Core Ops, SparseCore 0:
  10.2 44.6 all-gather.34
  56.5 22.4 all-gather.22
  80.5 22.5 all-gather.24
  111.8 23.4 all-gather.26
  137.2 47.5 all-gather.36
  186.3 21.8 all-gather.28
  209.8 34.5 all-gather.30
  343.0 33.2 all-gather.32
  742.4 287.0 all-reduce.37
  1031.8 19.2 reduce-scatter.37
  1055.5 63.8 reduce-scatter.27
  1123.2 62.5 reduce-scatter.29
  1190.2 62.4 reduce-scatter.31
  1256.5 62.4 reduce-scatter.25
  1323.4 66.8 reduce-scatter.33
  1394.7 66.7 reduce-scatter.35
where the time goes:
time: 1480 us; the launch traced here: 1470 us
  waiting for transfers between devices  611 us (41%)
  blocking collectives  361 us (24%)
  matrix products  186 us (13%)
  other arithmetic  129 us (9%)
  local copies, waits for them, and re-layouts  126 us (9%)
  starting transfers between devices  32.7 us (2%)
  between operations  17.6 us (1%)
    unnamed x17, waiting for transfers between devices  269 us
    unnamed x4, blocking collectives  110 us
    reduce_scatter x1, waiting for transfers between devices, on_device(): lax.psum_scatter(first_pass[8], 'dp', scatter_dimension=0, tiled=True)  71.2 us
    reduce_scatter x1, waiting for transfers between devices, on_device(): lax.psum_scatter(first_pass[10], 'dp', scatter_dimension=0, tiled=True)  71.1 us
    reduce_scatter x1, waiting for transfers between devices, on_device(): lax.psum_scatter(first_pass[6], 'dp', scatter_dimension=0, tiled=True)  66.9 us
    reduce_scatter x1, waiting for transfers between devices, on_device(): lax.psum_scatter(first_pass[0], 'dp', scatter_dimension=0, tiled=True)  66.4 us
    unnamed x10, other arithmetic  59.5 us
    unnamed x214, local copies, waits for them, and re-layouts  52.1 us
  transfers between devices with their start and end apart: 24, of which 10 were waited for; matrix products, arithmetic and copies ran while one was open for 17% of the time, Pallas kernels for 0%

commit v1 on v0

--- a/solution.py
+++ b/solution.py
@@ -4,16 +4,515 @@
 import jax
 import jax.numpy as jnp
 from jax import lax
+from jax.experimental import pallas as pl
+from jax.experimental.pallas import tpu as pltpu
 from jax.sharding import PartitionSpec as P
 
 HEAD_DIM = 64
 MODEL_WIDTH = 1024
 SEGS = 4
-
-
 EPSILON = 1e-06
 NEGATIVE = -1e30
 HIGHEST = lax.Precision.HIGHEST
+F32 = jnp.float32
+BF16 = jnp.bfloat16
+LANES = 128
+
+
+class Mover:
+    def __init__(self, send_sems, recv_sems, local_sems):
+        self.send_sems, self.recv_sems, self.local_sems = send_sems, recv_sems, local_sems
+        self.count = self.local_count = 0
+        self.sent = []
+
+    def send(self, source, target, device):
+        slot = self.count
+        self.count += 1
+        copy = pltpu.make_async_remote_copy(
+            src_ref=source,
+            dst_ref=target,
+            send_sem=self.send_sems.at[slot],
+            recv_sem=self.recv_sems.at[slot],
+            device_id=device,
+            device_id_type=pl.DeviceIdType.MESH,
+        )
+        copy.start()
+        self.sent.append(copy)
+        return copy
+
+    def local(self, source, target):
+        slot = self.local_count
+        self.local_count += 1
+        copy = pltpu.make_async_copy(source, target, self.local_sems.at[slot])
+        copy.start()
+        return copy
+
+    def finish(self):
+        for copy in self.sent:
+            copy.wait_send()
+
+
+class Place:
+    def __init__(self, depth):
+        dp, seq = lax.axis_index("dp"), lax.axis_index("seq")
+        self.depth = depth
+        self.z, self.y = dp // 2, dp % 2
+        self.x, self.c = seq // 2, seq % 2
+        self.seq = seq
+        self.index = dp * 4 + seq
+
+    def at(self, z, y, x, c):
+        return {"dp": z * 2 + y, "seq": x * 2 + c}
+
+    def core(self):
+        return self.at(self.z, self.y, self.x, 1 - self.c)
+
+    def across_x(self):
+        return self.at(self.z, self.y, 1 - self.x, self.c)
+
+    def across_y(self):
+        return self.at(self.z, 1 - self.y, self.x, self.c)
+
+    def ahead(self, step):
+        return (self.z + step) % self.depth
+
+    def along_z(self, step):
+        return self.at(self.ahead(step), self.y, self.x, self.c)
+
+    def row_peer(self, step):
+        return {"dp": self.z * 2 + self.y, "seq": (self.seq + step) % 4}
+
+    def enter(self):
+        barrier = pltpu.get_barrier_semaphore()
+        peers = [self.row_peer(step) for step in (1, 2, 3)] + [self.across_y()]
+        peers += [self.along_z(step) for step in range(1, self.depth)]
+        for peer in peers:
+            pl.semaphore_signal(barrier, 1, device_id=peer, device_id_type=pl.DeviceIdType.MESH)
+        pl.semaphore_wait(barrier, len(peers))
+
+
+def lanes_of(shape, axis=1):
+    return lax.broadcasted_iota(jnp.int32, shape, axis)
+
+
+def frame_segments(lens, first_row, rows, width):
+    position = lanes_of((rows, width), 0) + first_row
+    first, second, third = lens[0, 0], lens[0, 0] + lens[0, 1], lens[0, 0] + lens[0, 1] + lens[0, 2]
+    segment = (
+        (position >= first).astype(jnp.int32)
+        + (position >= second).astype(jnp.int32)
+        + (position >= third).astype(jnp.int32)
+    )
+    start = jnp.where(
+        segment == 0, 0, jnp.where(segment == 1, first, jnp.where(segment == 2, second, third))
+    )
+    return segment, position - start
+
+
+def three_parts(values):
+    high = values.astype(BF16).astype(F32)
+    rest = values - high
+    middle = rest.astype(BF16).astype(F32)
+    return high, middle, (rest - middle).astype(BF16).astype(F32)
+
+
+def swap_halves(values, lane):
+    return jnp.where(
+        lane % HEAD_DIM < HEAD_DIM // 2, pltpu.roll(values, 96, 1), pltpu.roll(values, 32, 1)
+    )
+
+
+def head_only(values, lane, head):
+    return jnp.where((lane >= HEAD_DIM) == bool(head), values.astype(F32), 0.0).astype(BF16)
+
+
+def across(left, right):
+    return lax.dot_general(left, right, (((1,), (1,)), ((), ())), preferred_element_type=F32)
+
+
+def product(left, right):
+    return jnp.dot(left, right, preferred_element_type=F32)
+
+
+def forward_kernel(
+    depth,
+    lens, times, frames, biases, wq, wk, wv, wo, up, down, mw,
+    att, oh, qs, ks, vs, lse, normed, wg, mods, cosr, sinr, bb, low, wo_all, up_all, down_all,
+    xall, mwst, tb, part, recva, suma, recvb, sumb, recvc, sumc, recvd, modh, bmat, mod3, qbias,
+    ka, va, qaug, send_sems, recv_sems, local_sems,
+):
+    here = Place(depth)
+    z, y, x, c, g = here.z, here.y, here.x, here.c, here.seq
+    span = frames.shape[0]
+    rows_all = span * 4
+    move = Mover(send_sems, recv_sems, local_sems)
+    steps_z = range(1, depth)
+
+    row = lanes_of((16, LANES), 0) % 4
+    own_times = jnp.where(
+        row == 0, times[0, 0], jnp.where(row == 1, times[0, 1], jnp.where(row == 2, times[0, 2], times[0, 3]))
+    )
+    tb[z, y] = own_times.astype(F32)
+    bb[z, y, x, c] = biases[...]
+    weights = (wq, wk, wv)
+    own_width = wg.shape[-1]
+    locals_first = [
+        move.local(weights[j].at[:, pl.ds(pl.multiple_of(g * own_width, LANES), own_width)], wg.at[j, z, y, g])
+        for j in range(3)
+    ]
+    strip = mw.shape[1] // 4
+    local_mw = [
+        move.local(mw.at[:, pl.ds(j * strip, strip)], mwst.at[pl.ds(j * 32, 32)]) for j in range(4)
+    ]
+    local_frames = move.local(frames, xall.at[g])
+    here.enter()
+
+    times_z = [move.send(tb.at[z, y], tb.at[z, y], here.along_z(k)) for k in steps_z]
+    bias_z = [move.send(bb.at[z, y, x, c], bb.at[z, y, x, c], here.along_z(k)) for k in steps_z]
+    qkv_row = []
+    for j in range(3):
+        for k in (1, 2, 3):
+            peer = (g + k) % 4
+            qkv_row.append(
+                move.send(
+                    weights[j].at[:, pl.ds(pl.multiple_of(peer * own_width, LANES), own_width)],
+                    wg.at[j, z, y, g],
+                    here.row_peer(k),
+                )
+            )
+    frames_x = move.send(frames, xall.at[g], here.across_x())
+    frames_core = move.send(frames, xall.at[g], here.core())
+    for copy in times_z:
+        copy.wait_recv()
+    times_y = move.send(tb.at[:, y], tb.at[:, y], here.across_y())
+    for copy in locals_first:
+        copy.wait()
+    for copy in qkv_row:
+        copy.wait_recv()
+    qkv_z = [
+        [move.send(wg.at[j, z, y], wg.at[j, z, y], here.along_z(k)) for k in steps_z] for j in range(3)
+    ]
+    for copy in bias_z:
+        copy.wait_recv()
+    bias_y = move.send(bb.at[:, y, x, c], bb.at[:, y, x, c], here.across_y())
+
+    times_y.wait_recv()
+    lane = lanes_of((16 * 2 * depth, LANES))
+    row = lanes_of((16 * 2 * depth, LANES), 0)
+    feature = here.index * 32 + lane % 32
+    halfway = MODEL_WIDTH // 2
+    frequency = jnp.exp((feature % halfway).astype(F32) * (-math.log(10000.0) / halfway))
+    angle = tb[...].reshape(16 * 2 * depth, LANES) * frequency
+    wave = jnp.where(feature < halfway, jnp.sin(angle), jnp.cos(angle))
+    gated = wave / (1.0 + jnp.exp(-wave))
+    low[...] = jnp.where(lane // 32 == (row % 16) // 4, gated, 0.0).astype(BF16)
+    for copy in local_mw:
+        copy.wait()
+    half = strip // 2
+    for side in range(2):
+        share = product(low[...], mwst[:, side * half : (side + 1) * half])
+        part[side] = share.astype(BF16).reshape(depth, 2, 16, half)
+    mod_core = move.send(part.at[1 - c], recva, here.core())
+    bias_y.wait_recv()
+    bias_x = move.send(bb.at[:, :, x, c], bb.at[:, :, x, c], here.across_x())
+
+    block = 128
+
+    def tables(step, carry):
+        rows = pl.ds(pl.multiple_of(step * block, block), block)
+        segment, relative = frame_segments(lens, step * block, block, LANES)
+        lane = lanes_of((block, LANES))
+        quarter = HEAD_DIM // 2
+        frequency = jnp.exp((lane % quarter).astype(F32) * (-math.log(10000.0) / quarter))
+        angle = relative.astype(F32) * frequency
+        cosr[rows, :] = jnp.cos(angle)
+        sine = jnp.sin(angle)
+        sinr[rows, :] = jnp.where(lane % HEAD_DIM < quarter, -sine, sine)
+        same = segment == lane
+        qaug[rows, :] = jnp.where((lane < SEGS) & jnp.logical_not(same), NEGATIVE, 0.0).astype(BF16)
+        keyside = jnp.where((lane < SEGS) & same, 1.0, jnp.where((lane >= 4) & (lane < 7), 1.0, 0.0))
+        for pair in range(2):
+            ka[pair, rows, LANES:] = keyside.astype(BF16)
+            va[pair, rows, LANES:] = jnp.where(lane < 3, 1.0, 0.0).astype(BF16)
+        return carry
+
+    lax.fori_loop(0, rows_all // (2 * block), tables, 0)
+    mod_core.wait_recv()
+    suma[...] = (part[c].astype(F32) + recva[...].astype(F32)).astype(BF16)
+    mod_y = move.send(suma.at[:, 1 - y], recvb, here.across_y())
+    bias_x.wait_recv()
+    bias_core = move.send(bb.at[:, :, :, c], bb.at[:, :, :, c], here.core())
+    lax.fori_loop(rows_all // (2 * block), rows_all // block, tables, 0)
+    mod_y.wait_recv()
+    sumb[...] = (suma[:, y].astype(F32) + recvb[...].astype(F32)).astype(BF16)
+    mod_z = [move.send(sumb.at[here.ahead(k)], recvc.at[k - 1], here.along_z(k)) for k in steps_z]
+    qkv_y = []
+    for j in range(3):
+        for copy in qkv_z[j]:
+            copy.wait_recv()
+        qkv_y.append(move.send(wg.at[j, :, y], wg.at[j, :, y], here.across_y()))
+    total = sumb[z].astype(F32)
+    for k in steps_z:
+        mod_z[k - 1].wait_recv()
+        total = total + recvc[k - 1].astype(F32)
+    sumc[...] = total
+    mod_x = move.send(sumc, recvd, here.across_x())
+
+    def first_leg(source, target):
+        own = move.local(source, target.at[z, y, x, c])
+        sends = [move.send(source, target.at[z, y, x, c], here.along_z(k)) for k in steps_z]
+        return own, sends
+
+    legs = {}
+    wo_top, wo_low = wo.at[pl.ds(0, 16)], wo.at[pl.ds(16, 16)]
+    wo_all_top, wo_all_low = wo_all.at[:, :, :, :, pl.ds(0, 16)], wo_all.at[:, :, :, :, pl.ds(16, 16)]
+    flows = [(wo_top, wo_all_top, 0), (wo_low, wo_all_low, 1), (up, up_all, 0), (down, down_all, 1)]
+    for number, (source, target, _) in enumerate(flows):
+        legs[number] = first_leg(source, target)
+
+    def second_leg(number):
+        _, target, order = flows[number]
+        own, sends = legs[number]
+        own.wait()
+        for copy in sends:
+            copy.wait_recv()
+        peer = here.across_x() if order else here.across_y()
+        legs[number] = move.send(target.at[:, y, x, c], target.at[:, y, x, c], peer)
+
+    def third_leg(number):
+        _, target, order = flows[number]
+        legs[number].wait_recv()
+        if order:
+            legs[number] = move.send(target.at[:, y, :, c], target.at[:, y, :, c], here.across_y())
+        else:
+            legs[number] = move.send(target.at[:, :, x, c], target.at[:, :, x, c], here.across_x())
+
+    def fourth_leg(number):
+        _, target, _ = flows[number]
+        legs[number].wait_recv()
+        legs[number] = move.send(target.at[:, :, :, c], target.at[:, :, :, c], here.core())
+
+    bias_core.wait_recv()
+    bmat[...] = bb[...].reshape(16 * 2 * depth * 2, LANES).astype(BF16)
+
+    place = lanes_of((LANES, own_width), 0)
+    column = lanes_of((LANES, own_width))
+    spread = jnp.where(column % 32 == place, 1.0, 0.0).astype(BF16)
+    held = product(bmat[pl.ds(pl.multiple_of(g * 64, 64), 64), :], spread)
+    brow, bcol = lanes_of((64, own_width), 0), lanes_of((64, own_width))
+    for j in range(3):
+        mine = (brow % 8 == j) & (brow // 8 == bcol // 32)
+        qbias[j : j + 1, :] = jnp.sum(jnp.where(mine, held, 0.0), axis=0, keepdims=True)
+
+    frames_x.wait_recv()
+    frames_on = move.send(xall.at[(g + 2) % 4], xall.at[(g + 2) % 4], here.core())
+    mod_x.wait_recv()
+    modh[c] = sumc[...] + recvd[...]
+    mod_last = move.send(modh.at[c], modh.at[c], here.core())
+
+    place = lanes_of((LANES, half), 0)
+    column = lanes_of((LANES, half))
+    spread_a = jnp.where(column % 192 == place, 1.0, 0.0).astype(BF16)
+    spread_b = jnp.where(column % 192 == place + LANES, 1.0, 0.0).astype(BF16)
+    brow, bcol = lanes_of((32, half), 0), lanes_of((32, half))
+    mod_last.wait_recv()
+    for q in range(8):
+        rows = bmat[q * 32 : (q + 1) * 32, :]
+        inside = brow // 8 == bcol // 192
+        terms = jnp.where(inside & (brow % 8 == 6), product(rows, spread_a), 0.0)
+        terms = terms + jnp.where(inside & (brow % 8 == 7), product(rows, spread_b), 0.0)
+        offset = jnp.sum(terms, axis=0, keepdims=True)
+        j, side = q // 2, q % 2
+        mods[0:4, q * half : (q + 1) * half] = modh[side, 4 * j : 4 * j + 4, :] + offset
+    mods[4:8, :] = jnp.zeros((4, mods.shape[1]), F32)
+    high, middle, rest = three_parts(mods[0:4, 0 : 2 * MODEL_WIDTH])
+    mod3[0:4, :] = high
+    mod3[4:8, :] = middle
+    mod3[8:12, :] = rest
+    mod3[12:16, :] = jnp.zeros((4, 2 * MODEL_WIDTH), F32)
+
+    def project_rows(step, carry):
+        rows = pl.ds(pl.multiple_of(step * block, block), block)
+        per = span // block
+        source = step // per
+        values = xall[source, pl.ds(pl.multiple_of((step % per) * block, block), block), :].astype(F32)
+        center = jnp.mean(values, axis=1, keepdims=True)
+        centered = values - center
+        variance = jnp.mean(centered * centered, axis=1, keepdims=True)
+        segment, _ = frame_segments(lens, step * block, block, 16)
+        slot = lanes_of((block, 16))
+        chosen = jnp.where((slot < 12) & (slot % 4 == segment), 1.0, 0.0).astype(BF16)
+        parts = mod3[...].astype(BF16)
+        shift = product(chosen, parts[:, :MODEL_WIDTH])
+        scale = product(chosen, parts[:, MODEL_WIDTH:])
+        result = (centered * lax.rsqrt(variance + EPSILON) * (1.0 + scale) + shift).astype(BF16)
+        normed[rows, :] = result
+        cosine, sine = cosr[rows, :], sinr[rows, :]
+        lane = lanes_of((block, LANES))
+        for j in range(3):
+            weight = wg[j].reshape(MODEL_WIDTH, own_width)
+            full = product(result, weight) + qbias[j : j + 1, :]
+            for pair in range(2):
+                piece = full[:, pair * LANES : (pair + 1) * LANES]
+                if j < 2:
+                    piece = piece * cosine + swap_halves(piece, lane) * sine
+                if j == 0:
+                    qs[pair, rows, :] = (piece.astype(BF16).astype(F32) * HEAD_DIM**-0.5).astype(BF16)
+                elif j == 1:
+                    ks[pair, rows, :] = piece.astype(BF16)
+                    ka[pair, rows, :LANES] = piece.astype(BF16)
+                else:
+                    vs[pair, rows, :] = piece.astype(BF16)
+                    va[pair, rows, :LANES] = piece.astype(BF16)
+        return carry
+
+    for copy in qkv_y:
+        copy.wait_recv()
+    local_frames.wait()
+    frames_core.wait_recv()
+    second_leg(0)
+    second_leg(1)
+    frames_on.wait_recv()
+    lax.fori_loop(0, rows_all // block, project_rows, 0)
+
+    tall = 256
+
+    def attend(pair, step):
+        rows = pl.ds(pl.multiple_of(step * tall, tall), tall)
+        query = qs[pair, rows, :]
+        lane = lanes_of((tall, LANES))
+        outs, sums = [], []
+        for head in range(2):
+            left = jnp.concatenate([head_only(query, lane, head), qaug[rows, :]], axis=1)
+            scores = across(left, ka[pair])
+            highest = jnp.max(scores, axis=1, keepdims=True)
+            mixed = product(jnp.exp(scores - highest).astype(BF16), va[pair])
+            total = mixed[:, LANES : LANES + 1]
+            outs.append(mixed[:, :LANES] / total)
+            sums.append(highest + jnp.log(total))
+        oh[pair, rows, :] = jnp.where(lane < HEAD_DIM, outs[0], outs[1]).astype(BF16)
+        before = jnp.zeros((tall, LANES), F32) if pair == 0 else lse[rows, :]
+        lse[rows, :] = jnp.where(
+            lane == 2 * pair, sums[0], jnp.where(lane == 2 * pair + 1, sums[1], before)
+        )
+
+    def attend_some(pair, first, last):
+        lax.fori_loop(first, last, lambda step, carry: (attend(pair, step), carry)[1], 0)
+
+    steps = rows_all // tall
+    arrivals = []
+    pair_locals = []
+
+    def deliver(pair):
+        columns = pl.ds(pl.multiple_of(g * own_width + pair * LANES, LANES), LANES)
+        pair_locals.append(
+            move.local(oh.at[pair, pl.ds(pl.multiple_of(g * span, span), span)], att.at[:, columns])
+        )
+        for k in (1, 2, 3):
+            peer = (g + k) % 4
+            arrivals.append(
+                move.send(
+                    oh.at[pair, pl.ds(pl.multiple_of(peer * span, span), span)],
+                    att.at[:, columns],
+                    here.row_peer(k),
+                )
+            )
+
+    attend_some(0, 0, steps // 2)
+    second_leg(2)
+    second_leg(3)
+    third_leg(0)
+    third_leg(1)
+    attend_some(0, steps // 2, steps)
+    deliver(0)
+    fourth_leg(0)
+    fourth_leg(1)
+    attend_some(1, 0, steps // 2)
+    third_leg(2)
+    third_leg(3)
+    attend_some(1, steps // 2, steps)
+    deliver(1)
+    fourth_leg(2)
+    fourth_leg(3)
+    for number in range(4):
+        legs[number].wait_recv()
+    for copy in arrivals:
+        copy.wait_recv()
+    for copy in pair_locals:
+        copy.wait()
+    move.finish()
+
+
+def forward_call(depth, span, own_rows, down_rows, hidden, args):
+    rows_all, own_width = 4 * span, MODEL_WIDTH // 4
+    half = 6 * MODEL_WIDTH // 8
+    vmem, anywhere, scalar = (
+        pl.BlockSpec(memory_space=pltpu.VMEM),
+        pl.BlockSpec(memory_space=pl.ANY),
+        pl.BlockSpec(memory_space=pltpu.SMEM),
+    )
+
+    def out(shape, dtype):
+        return jax.ShapeDtypeStruct(shape, dtype)
+
+    outs = [
+        (out((span, MODEL_WIDTH), BF16), anywhere),
+        (out((2, rows_all, LANES), BF16), vmem),
+        (out((2, rows_all, LANES), BF16), vmem),
+        (out((2, rows_all, LANES), BF16), vmem),
+        (out((2, rows_all, LANES), BF16), vmem),
+        (out((rows_all, LANES), F32), vmem),
+        (out((rows_all, MODEL_WIDTH), BF16), vmem),
+        (out((3, depth, 2, 4, own_rows, own_width), BF16), vmem),
+        (out((8, 6 * MODEL_WIDTH), F32), vmem),
+        (out((rows_all, LANES), F32), vmem),
+        (out((rows_all, LANES), F32), vmem),
+        (out((depth, 2, 2, 2, 8, LANES), F32), vmem),
+        (out((32 * depth, LANES), BF16), vmem),
+        (out((depth, 2, 2, 2, own_rows, MODEL_WIDTH), BF16), anywhere),
+        (out((depth, 2, 2, 2, own_rows, hidden), BF16), anywhere),
+        (out((depth, 2, 2, 2, down_rows, MODEL_WIDTH), BF16), anywhere),
+    ]
+    scratch = [
+        pltpu.VMEM((4, span, MODEL_WIDTH), BF16),
+        pltpu.VMEM((LANES, 2 * half), BF16),
+        pltpu.VMEM((depth, 2, 16, LANES), F32),
+        pltpu.VMEM((2, depth, 2, 16, half), BF16),
+        pltpu.VMEM((depth, 2, 16, half), BF16),
+        pltpu.VMEM((depth, 2, 16, half), BF16),
+        pltpu.VMEM((depth, 16, half), BF16),
+        pltpu.VMEM((depth, 16, half), BF16),
+        pltpu.VMEM((depth - 1, 16, half), BF16),
+        pltpu.VMEM((16, half), F32),
+        pltpu.VMEM((16, half), F32),
+        pltpu.VMEM((2, 16, half), F32),
+        pltpu.VMEM((64 * depth, LANES), BF16),
+        pltpu.VMEM((16, 2 * MODEL_WIDTH), F32),
+        pltpu.VMEM((8, own_width), F32),
+        pltpu.VMEM((2, rows_all, 2 * LANES), BF16),
+        pltpu.VMEM((2, rows_all, 2 * LANES), BF16),
+        pltpu.VMEM((rows_all, LANES), BF16),
+        pltpu.SemaphoreType.DMA((96,)),
+        pltpu.SemaphoreType.DMA((96,)),
+        pltpu.SemaphoreType.DMA((24,)),
+    ]
+    return pl.pallas_call(
+        partial(forward_kernel, depth),
+        out_shape=[shape for shape, _ in outs],
+        in_specs=[scalar, scalar, anywhere, vmem] + [anywhere] * 7,
+        out_specs=[spec for _, spec in outs],
+        scratch_shapes=scratch,
+        compiler_params=pltpu.CompilerParams(
+            collective_id=0, has_side_effects=True, vmem_limit_bytes=56 * 1024 * 1024
+        ),
+        cost_estimate=pl.CostEstimate(flops=8 * 10**9, bytes_accessed=40 * 10**6, transcendentals=10**7),
+    )(*args)
+
+
+def bias_block(query_bias, key_bias, value_bias, output_bias, up_bias, down_bias, modulation_bias):
+    rows = [query_bias, key_bias, value_bias, output_bias, up_bias, down_bias]
+    rows += [modulation_bias[:LANES], modulation_bias[LANES:]]
+    return jnp.stack([jnp.pad(row, (0, LANES - row.shape[0])) for row in rows]).astype(F32)
 
 
 def modulated_norm(values, shift_part, scale_part):
@@ -499,9 +998,310 @@
     )
 
 
+def on_device_fast(frames, output_gradient, segment_lengths, time_index, query_weight, query_bias, key_weight,
+                   key_bias, value_weight, value_bias, output_projection, output_bias, up_weight, up_bias,
+                   down_weight, down_bias, modulation_weight, modulation_bias):
+    narrow_count = lax.axis_size("seq")
+    wide_count = lax.axis_size("dp")
+    seq_index = lax.axis_index("seq")
+    row_count, span_frames, width_total = frames.shape
+    row_length = span_frames * narrow_count
+    block_rows = min(512, row_length)
+    block_count = row_length // block_rows
+    blocks = bias_block(query_bias, key_bias, value_bias, output_bias, up_bias, down_bias, modulation_bias)
+    (att, oh, qs, ks, vs, lse, normed_all, wg, mods, cosr, sinr, bb, low, wo_all, up_all, down_all) = forward_call(
+        wide_count // 2, span_frames, query_weight.shape[0], down_weight.shape[0], up_weight.shape[1],
+        (segment_lengths, time_index, frames[0], blocks, query_weight, key_weight, value_weight,
+         output_projection, up_weight, down_weight, modulation_weight))
+    gathered_bias = bb.reshape(-1, 8, LANES)
+    full_output_bias = gathered_bias[:, 3, : output_bias.shape[0]].reshape(-1)
+    full_up_bias = gathered_bias[:, 4, : up_bias.shape[0]].reshape(-1)
+    full_down_bias = gathered_bias[:, 5, : down_bias.shape[0]].reshape(-1)
+    full_output = wo_all.reshape(width_total, width_total)
+    full_up = up_all.reshape(width_total, -1)
+    full_down = down_all.reshape(-1, width_total)
+    lifted = [lift_up(m) for m in (query_weight, key_weight, value_weight)]
+    lifted = [lax.all_gather(m, "dp", axis=0, tiled=True) for m in lifted]
+    full_query, full_key, full_value = [settle(lax.all_gather(m, "seq", axis=1, tiled=True)) for m in lifted]
+    local_positions = seq_index * span_frames + jnp.arange(span_frames, dtype=jnp.int32)
+    local_onehot, local_relative = segment_layout(segment_lengths, local_positions)
+    row_segment = segment_numbers(segment_lengths, jnp.arange(row_length, dtype=jnp.int32))
+    cosines, sines_table = rope_tables(local_relative)
+    turning = partial(rotate, cosines=cosines, sines_table=sines_table)
+    owned_rows = modulation_weight.shape[0]
+    owned_start = (lax.axis_index("dp") * narrow_count + seq_index) * owned_rows
+    every_time = lax.all_gather(time_index, "dp", axis=0, tiled=True)
+    every_low = jax.nn.silu(time_features(every_time)).astype(jnp.bfloat16)
+    owned_low = lax.dynamic_slice_in_dim(every_low, owned_start, owned_rows, 2)
+    modulation = mods[None, :SEGS]
+    per_frame = jnp.einsum("rls,rsc->rlc", local_onehot, modulation, precision=HIGHEST)
+    shift_one, scale_one, gate_one, shift_two, scale_two, gate_two = jnp.split(per_frame, 6, axis=-1)
+    inputs = frames.astype(jnp.float32)
+    normed, norm_back = jax.vjp(modulated_norm, inputs, shift_one, scale_one)
+    normed_low = normed.astype(jnp.bfloat16)
+    zero = jnp.zeros(inputs.shape, jnp.float32)
+    _, query_back = jax.vjp(turning, zero)
+    _, key_back = jax.vjp(turning, zero)
+    local_heads = full_query.shape[1] // narrow_count // HEAD_DIM
+    head_shape = (row_count, row_length, local_heads, HEAD_DIM)
+    side = lambda t: t.transpose(1, 0, 2).reshape(head_shape)
+    queries, keys_all, values_all = side(qs * 8), side(ks), side(vs)
+    scaling = HEAD_DIM ** (-0.5)
+    positions_all = jnp.arange(row_count * block_count, dtype=jnp.int32)
+
+    def fetch_block(position):
+        row_index = position // block_count
+        start_row = position % block_count * block_rows
+        key_row = lax.dynamic_index_in_dim(keys_all, row_index, 0, keepdims=False)
+        value_row = lax.dynamic_index_in_dim(values_all, row_index, 0, keepdims=False)
+        segment_row = lax.dynamic_index_in_dim(row_segment, row_index, 0, keepdims=False)
+        query_block = lax.dynamic_slice_in_dim(
+            lax.dynamic_index_in_dim(queries, row_index, 0, keepdims=False),
+            start_row,
+            block_rows,
+            0,
+        )
+        segment_block = lax.dynamic_slice_in_dim(segment_row, start_row, block_rows, 0)
+        scores = (
+            jnp.einsum("bhd,khd->hbk", query_block, key_row, preferred_element_type=jnp.float32)
+            * scaling
+        )
+        scores = jnp.where((segment_block[:, None] == segment_row[None, :])[None], scores, NEGATIVE)
+        return (row_index, start_row, query_block, key_row, value_row, scores)
+
+    logsums = lse[:, :local_heads].T.reshape(local_heads, block_count, block_rows).transpose(1, 0, 2)
+    attention_frames = att[None]
+    branch = project(attention_frames, full_output, full_output_bias)
+    middle = inputs + gate_one * branch
+    normed_two, norm_two_back = jax.vjp(modulated_norm, middle, shift_two, scale_two)
+    normed_two_low = normed_two.astype(jnp.bfloat16)
+    hidden = project(normed_two_low, full_up, full_up_bias)
+    activated, gelu_back = jax.vjp(gelu_tanh, hidden)
+    activated_low = activated.astype(jnp.bfloat16)
+    branch_two = project(activated_low, full_down, full_down_bias)
+    layer_output = (middle + gate_two * branch_two).astype(jnp.bfloat16)
+    cotangent = output_gradient.astype(jnp.float32)
+    grad_branch_two = (gate_two * cotangent).astype(jnp.bfloat16)
+    grad_gate_two = cotangent * branch_two
+    grad_activated = project_back(grad_branch_two, full_down)
+    grad_hidden = gelu_back(grad_activated)[0].astype(jnp.bfloat16)
+    grad_normed_two = project_back(grad_hidden, full_up)
+    grad_middle_part, grad_shift_two, grad_scale_two = norm_two_back(grad_normed_two)
+    grad_middle = cotangent + grad_middle_part
+    grad_gate_one = grad_middle * branch
+    grad_branch = (gate_one * grad_middle).astype(jnp.bfloat16)
+    grad_attention = project_back(grad_branch, full_output).astype(jnp.bfloat16)
+    grad_heads = lax.all_to_all(grad_attention, "seq", split_axis=2, concat_axis=1, tiled=True)
+    grad_outputs = grad_heads.reshape(head_shape)
+
+    def backward_block(running, pair_inputs):
+        grad_keys, grad_values = running
+        position, logsum = pair_inputs
+        row_index, start_row, query_block, key_row, value_row, scores = fetch_block(position)
+        grad_block = lax.dynamic_slice_in_dim(
+            lax.dynamic_index_in_dim(grad_outputs, row_index, 0, keepdims=False),
+            start_row,
+            block_rows,
+            0,
+        )
+        probabilities = jnp.exp(scores - logsum[..., None])
+        grad_probabilities = jnp.einsum(
+            "bhd,khd->hbk", grad_block, value_row, preferred_element_type=jnp.float32
+        )
+        delta_sum = jnp.sum(probabilities * grad_probabilities, axis=2, keepdims=True)
+        grad_scores = (probabilities * (grad_probabilities - delta_sum)).astype(jnp.bfloat16)
+        grad_query_block = (
+            jnp.einsum("hbk,khd->bhd", grad_scores, key_row, preferred_element_type=jnp.float32)
+            * scaling
+        )
+        key_part = (
+            jnp.einsum("hbk,bhd->khd", grad_scores, query_block, preferred_element_type=jnp.float32)
+            * scaling
+        )
+        value_part = jnp.einsum(
+            "hbk,bhd->khd",
+            probabilities.astype(jnp.bfloat16),
+            grad_block,
+            preferred_element_type=jnp.float32,
+        )
+        grad_keys = lax.dynamic_update_index_in_dim(
+            grad_keys,
+            lax.dynamic_index_in_dim(grad_keys, row_index, 0, keepdims=False) + key_part,
+            row_index,
+            0,
+        )
+        grad_values = lax.dynamic_update_index_in_dim(
+            grad_values,
+            lax.dynamic_index_in_dim(grad_values, row_index, 0, keepdims=False) + value_part,
+            row_index,
+            0,
+        )
+        return (
+            (grad_keys, grad_values),
+            grad_query_block.astype(jnp.bfloat16).reshape(block_rows, -1),
+        )
+
+    zero_heads = jnp.zeros(head_shape, jnp.float32)
+    (grad_keys_all, grad_values_all), grad_query_blocks = lax.scan(
+        backward_block, (zero_heads, zero_heads), (positions_all, logsums)
+    )
+    flat_shape = (row_count, row_length, -1)
+    grad_query_frames, grad_key_frames, grad_value_frames = (
+        lax.all_to_all(
+            grad_query_blocks.reshape(flat_shape), "seq", split_axis=1, concat_axis=2, tiled=True
+        ),
+        lax.all_to_all(
+            grad_keys_all.reshape(flat_shape).astype(jnp.bfloat16),
+            "seq",
+            split_axis=1,
+            concat_axis=2,
+            tiled=True,
+        ),
+        lax.all_to_all(
+            grad_values_all.reshape(flat_shape).astype(jnp.bfloat16),
+            "seq",
+            split_axis=1,
+            concat_axis=2,
+            tiled=True,
+        ),
+    )
+    grad_query_pre = query_back(grad_query_frames.astype(jnp.float32))[0].astype(jnp.bfloat16)
+    grad_key_pre = key_back(grad_key_frames.astype(jnp.float32))[0].astype(jnp.bfloat16)
+    grad_normed = (
+        project_back(grad_query_pre, full_query)
+        + project_back(grad_key_pre, full_key)
+        + project_back(grad_value_frames, full_value)
+    )
+    grad_inputs_part, grad_shift_one, grad_scale_one = norm_back(grad_normed)
+    frames_grad = (grad_middle + grad_inputs_part).astype(jnp.bfloat16)
+    grad_per_frame = jnp.concatenate(
+        [
+            grad_shift_one,
+            grad_scale_one,
+            grad_gate_one,
+            grad_shift_two,
+            grad_scale_two,
+            grad_gate_two,
+        ],
+        axis=-1,
+    )
+    grad_modulation = jnp.einsum("rls,rlc->rsc", local_onehot, grad_per_frame, precision=HIGHEST)
+    gradients = (
+        weight_gradient(normed_low, grad_query_pre),
+        bias_gradient(grad_query_pre),
+        weight_gradient(normed_low, grad_key_pre),
+        bias_gradient(grad_key_pre),
+        weight_gradient(normed_low, grad_value_frames),
+        bias_gradient(grad_value_frames),
+        weight_gradient(attention_frames, grad_branch),
+        bias_gradient(grad_branch),
+        weight_gradient(normed_two_low, grad_hidden),
+        bias_gradient(grad_hidden),
+        weight_gradient(activated_low, grad_branch_two),
+        bias_gradient(grad_branch_two),
+        jnp.sum(grad_modulation, axis=(0, 1)),
+    )
+    row_total = lax.psum(grad_modulation.astype(jnp.bfloat16), "seq").astype(jnp.float32)
+    every_grad = lax.all_gather(row_total.astype(jnp.bfloat16), "dp", axis=0, tiled=True).astype(
+        row_total.dtype
+    )
+    modulation_weight_grad = jnp.einsum(
+        "rsd,rsc->dc", owned_low.astype(jnp.float32), every_grad, precision=HIGHEST
+    )
+    spreaded = [spread(member, wide_count, narrow_count) for member in gradients]
+    first_pass = (
+        lax.psum_scatter(
+            spreaded[0].astype(jnp.bfloat16), "seq", scatter_dimension=1, tiled=True
+        ).astype(jnp.float32),
+        lax.psum_scatter(
+            spreaded[1].astype(jnp.bfloat16), "seq", scatter_dimension=1, tiled=True
+        ).astype(jnp.float32),
+        lax.psum_scatter(
+            spreaded[2].astype(jnp.bfloat16), "seq", scatter_dimension=1, tiled=True
+        ).astype(jnp.float32),
+        lax.psum_scatter(
+            spreaded[3].astype(jnp.bfloat16), "seq", scatter_dimension=1, tiled=True
+        ).astype(jnp.float32),
+        lax.psum_scatter(
+            spreaded[4].astype(jnp.bfloat16), "seq", scatter_dimension=1, tiled=True
+        ).astype(jnp.float32),
+        lax.psum_scatter(
+            spreaded[5].astype(jnp.bfloat16), "seq", scatter_dimension=1, tiled=True
+        ).astype(jnp.float32),
+        lax.psum_scatter(
+            spreaded[6].astype(jnp.bfloat16), "seq", scatter_dimension=1, tiled=True
+        ).astype(jnp.float32),
+        lax.psum_scatter(
+            spreaded[7].astype(jnp.bfloat16), "seq", scatter_dimension=1, tiled=True
+        ).astype(jnp.float32),
+        lax.psum_scatter(
+            spreaded[8].astype(jnp.bfloat16), "seq", scatter_dimension=1, tiled=True
+        ).astype(jnp.float32),
+        lax.psum_scatter(
+            spreaded[9].astype(jnp.bfloat16), "seq", scatter_dimension=1, tiled=True
+        ).astype(jnp.float32),
+        lax.psum_scatter(
+            spreaded[10].astype(jnp.bfloat16), "seq", scatter_dimension=1, tiled=True
+        ).astype(jnp.float32),
+        lax.psum_scatter(
+            spreaded[11].astype(jnp.bfloat16), "seq", scatter_dimension=1, tiled=True
+        ).astype(jnp.float32),
+        lax.psum_scatter(
+            spreaded[12].astype(jnp.bfloat16), "seq", scatter_dimension=1, tiled=True
+        ).astype(jnp.float32),
+    )
+    second_pass = (
+        lax.psum_scatter(first_pass[0], "dp", scatter_dimension=0, tiled=True),
+        lax.psum_scatter(first_pass[1], "dp", scatter_dimension=0, tiled=True),
+        lax.psum_scatter(first_pass[2], "dp", scatter_dimension=0, tiled=True),
+        lax.psum_scatter(first_pass[3], "dp", scatter_dimension=0, tiled=True),
+        lax.psum_scatter(first_pass[4], "dp", scatter_dimension=0, tiled=True),
+        lax.psum_scatter(first_pass[5], "dp", scatter_dimension=0, tiled=True),
+        lax.psum_scatter(first_pass[6], "dp", scatter_dimension=0, tiled=True),
+        lax.psum_scatter(first_pass[7], "dp", scatter_dimension=0, tiled=True),
+        lax.psum_scatter(first_pass[8], "dp", scatter_dimension=0, tiled=True),
+        lax.psum_scatter(first_pass[9], "dp", scatter_dimension=0, tiled=True),
+        lax.psum_scatter(first_pass[10], "dp", scatter_dimension=0, tiled=True),
+        lax.psum_scatter(first_pass[11], "dp", scatter_dimension=0, tiled=True),
+        lax.psum_scatter(first_pass[12], "dp", scatter_dimension=0, tiled=True),
+    )
+    reduced = [unpack(member) for member in second_pass]
+    return (
+        layer_output,
+        frames_grad,
+        reduced[0],
+        reduced[1],
+        reduced[2],
+        reduced[3],
+        reduced[4],
+        reduced[5],
+        reduced[6],
+        reduced[7],
+        reduced[8],
+        reduced[9],
+        reduced[10],
+        reduced[11],
+        modulation_weight_grad,
+        reduced[12],
+    )
+
+
+def fits(mesh, frames, *parameters):
+    dp, seq = mesh.shape["dp"], mesh.shape["seq"]
+    rows = parameters[3].shape[0] // (dp * seq)
+    return seq == 4 and dp % 2 == 0 and rows == 32 and frames.shape[0] == dp
+
+
 def solution(mesh):
+    def run(*arrays):
+        return mapped(mesh, on_device_fast if fits(mesh, *arrays) else on_device)(*arrays)
+
+    return run
+
+
+def mapped(mesh, body):
     return jax.shard_map(
-        on_device,
+        body,
         mesh=mesh,
         in_specs=(
             P("dp", "seq", None),

time: 1480 us -> 1290 us (0.87)
  blocking collectives: 361 us -> 201 us
  Pallas kernels: 0 us -> 129 us
  local copies, waits for them, and re-layouts: 126 us -> 80.3 us
  other arithmetic: 129 us -> 90.3 us
  waiting for transfers between devices: 611 us -> 578 us
  matrix products: 186 us -> 166 us
  starting transfers between devices: 32.7 us -> 16.8 us
    pallas_call x0 -> x1, Pallas kernels: none -> 129 us  [forward_call(): pl.pallas_call(partial(forward_kernel, depth), out_shape=[shape for shape...]
    all_gather x13 -> x5, blocking collectives: 240 us -> 156 us  [the longest x3 104 us: on_device_fast(): lifted = [lax.all_gather(m, 'dp', axis=0, tiled=True) for m in lifted]]
    unnamed x4 -> x2, blocking collectives: 110 us -> 45.1 us
    unnamed x214 -> x146, local copies, waits for them, and re-layouts: 52.1 us -> 25.5 us
    unnamed x10 -> x6, other arithmetic: 59.5 us -> 35.1 us
    reduce_scatter x7, waiting for transfers between devices: 321 us -> 301 us  [the longest x1 71.1 us: on_device_fast(): lax.psum_scatter(first_pass[8], 'dp', scatter_dimension=0, tiled=True)]
    all_to_all x8 -> x4, waiting for transfers between devices: 21.2 us -> 4.23 us  [the longest x1 4.22 us: on_device_fast(): lax.all_to_all(grad_values_all.reshape(flat_shape).astype(jnp.bfloat16),...]
    all_to_all x8 -> x4, starting transfers between devices: 31.6 us -> 16.2 us  [the longest x1 4.2 us: on_device_fast(): lax.all_to_all(grad_attention, 'seq', split_axis=2, concat_axis=1, tiled=...]
  transfers between devices with their start and end apart: 24 -> 15, of which waited for: 10 -> 7; matrix products, arithmetic and copies ran while one was open for 17% -> 24% of each run, Pallas kernels for 0% -> 10%
where the time goes in v1:
time: 1290 us; the launch traced here: 1280 us
  waiting for transfers between devices  578 us (45%)
  blocking collectives  201 us (16%)
  matrix products  166 us (13%)
  Pallas kernels  129 us (10%)
  other arithmetic  90.3 us (7%)
  local copies, waits for them, and re-layouts  80.3 us (6%)
  starting transfers between devices  16.8 us (1%)
  between operations  15.1 us (1%)
    unnamed x12, waiting for transfers between devices  273 us
    pallas_call x1, Pallas kernels, forward_call(): pl.pallas_call(partial(forward_kernel, depth), out_shape=[shape for shape...  129 us
    all_gather x3, blocking collectives, on_device_fast(): lifted = [lax.all_gather(m, 'dp', axis=0, tiled=True) for m in lifted]  104 us
    reduce_scatter x1, waiting for transfers between devices, on_device_fast(): lax.psum_scatter(first_pass[8], 'dp', scatter_dimension=0, tiled=True)  71.1 us
    reduce_scatter x1, waiting for transfers between devices, on_device_fast(): lax.psum_scatter(first_pass[10], 'dp', scatter_dimension=0, tiled=True)  71.1 us
    reduce_scatter x1, waiting for transfers between devices, on_device_fast(): lax.psum_scatter(first_pass[4], 'dp', scatter_dimension=0, tiled=True)  66.9 us
    reduce_scatter x1, waiting for transfers between devices, on_device_fast(): lax.psum_scatter(first_pass[6], 'dp', scatter_dimension=0, tiled=True)  66.4 us
    unnamed x2, blocking collectives  45.1 us
  transfers between devices with their start and end apart: 15, of which 7 were waited for; matrix products, arithmetic and copies ran while one was open for 24% of the time, Pallas kernels for 10%

profile of v1, /device:TPU:0, one launch (start us, length us, event | category | flops | bytes accessed | tf_op | source)
XLA Modules:
  0.0 1279.0 jit_solution(13391672605300563016)
XLA Ops:
  7.3 35.4 %all-gather.1 = bf16[256,1024]{1,0:T(8,128)(2,1)} all-gather(bf16[32,1024]{1,0:T(8,128)(2,1)} %wk.1), channel_id=3, replica_groups=mesh['dp'=8,'seq'=4] {'dp'}, dimensions={0}, use_global_device_ids=true | all-gather | bytes 589824 | tf_op jit(solution)/shard_map/all_gather | solution.py:1024
  42.8 33.5 %all-gather = bf16[256,1024]{1,0:T(8,128)(2,1)} all-gather(bf16[32,1024]{1,0:T(8,128)(2,1)} %wq.1), channel_id=2, replica_groups=mesh['dp'=8,'seq'=4] {'dp'}, dimensions={0}, use_global_device_ids=true | all-gather | bytes 589824 | tf_op jit(solution)/shard_map/all_gather | solution.py:1024
  77.2 128.6 %shard_map.297 = (bf16[384,1024]{1,0:T(8,128)(2,1)}, bf16[2,1536,128]{2,1,0:T(8,128)(2,1)}, bf16[2,1536,128]{2,1,0:T(8,128)(2,1)}, bf16[2,1536,128]{2,1,0:T(8,12...) custom-call(s32[1,4]{1,0:T(1,128)} %lens.1, ...), custom_call_target="tpu_custom_call" | custom-call | flops 8000000000 | bytes 40000000 | tf_op jit(solution)/shard_map/pallas_call | solution.py:499
  263.3 35.1 %all-gather.2 = bf16[256,1024]{1,0:T(8,128)(2,1)} all-gather(bf16[32,1024]{1,0:T(8,128)(2,1)S(1)} %copy-done.42), channel_id=4, replica_groups=mesh['dp'=8,'seq'=4] {'dp'}, dimensions={0}, use_global_device_ids=true | all-gather | bytes 589824 | tf_op jit(solution)/shard_map/all_gather | solution.py:1024
  321.2 115.4 %while.16 = (s32[]{:T(128)}, f32[1,1536,4,64]{1,3,2,0:T(8,128)}, f32[1,1536,4,64]{1,3,2,0:T(8,128)}, bf16[3,512,256]{2,1,0:T(8,128)(2,1)}, s32[3]{0:T(128)S(1)},...) while((s32[]{:T(128)}, f32[1,1536,4,64]{1,3,2,0:T(8,128)}, ...), condition=%wide.region_9.10_spmd, body=%wide.region_7.9_spmd.sunk | while | flops 2043803648 | bytes 232850480 | solution.py:1145
  329.5 7.7 multiply_reduce_fusion.4
  352.2 7.4 fusion.175
  368.0 7.7 multiply_reduce_fusion.4
  390.7 7.4 fusion.175
  406.4 7.7 multiply_reduce_fusion.4
  439.3 8.1 reduce.39
  461.0 8.8 copy.318
  469.8 8.1 reduce.40
  490.3 8.1 reduce.38
  567.6 272.7 %all-reduce.35.cloned.1.call-done = (bf16[8,4,32,1024]{3,2,1,0:T(8,128)(2,1)}, bf16[8,4,32,1024]{3,2,1,0:T(8,128)(2,1)}, bf16[8,4,32,1024]{3,2,1,0:T(8,128)(2,1)...) async-done(((bf16[8,4,32,1024]{3,2,1,0:T(8,128)(2,1)}, bf16[8,4,32,1024]{3,2,1,0:T(8,128)(2,1)}, ...) | async-done | bytes 16777232
  859.3 20.4 %all-gather.3 = s32[8,1,4]{2,1,0:T(1,128)S(1)} all-gather(s32[1,1,4]{2,1,0:T(1,128)S(1)} %bitcast.419), channel_id=1, replica_groups=mesh['dp'=8,'seq'=4] {'dp'}, dimensions={0}, use_global_device_ids=true | all-gather | bytes 144 | tf_op jit(solution)/shard_map/all_gather | solution.py:1033
  881.0 11.7 all-reduce.31
  896.7 31.3 %all_gather.31 = bf16[8,4,6144]{2,1,0:T(4,128)(2,1)S(1)} all-gather(bf16[1,4,6144]{2,1,0:T(4,128)(2,1)S(1)} %get-tuple-element.218), channel_id=1, replica_groups=mesh['dp'=8,'seq'=4] {'dp'}, dimensions={0}, use_global_device_ids=true | all-gather | bytes 442368 | tf_op jit(solution)/shard_map/all_gather | solution.py:1205
  930.0 33.4 %all-reduce.30 = (f32[8,1,32]{2,1,0:T(1,128)S(1)}, f32[8,1,32]{2,1,0:T(1,128)S(1)}, f32[8,1,32]{2,1,0:T(1,128)S(1)}, f32[8,1,32]{2,1,0:T(1,128)S(1)}, f32[8,1,64...) all-reduce(f32[8,1,32]{2,1,0:T(1,128)S(1)} %bitcast.417, ...), channel_id=8, replica_groups=mesh['dp'=8,'seq'=4] {'dp'}, use_global_device_ids=true, to_apply=%region_19.20.clone | all-reduce | flops 3328 | bytes 26624
  970.9 25.8 %reduce-scatter.28.cloned.1.call-done = f32[1,1,32,1024]{3,2,1,0:T(8,128)} async-done(((f32[8,1,32,1024]{3,2,1,0:T(8,128)}), f32[1,1,32,1024]{3,2,1,0:T(8,128)}) %reduce-scatter.28.cloned.1.call-update) | async-done | bytes 131088 | tf_op jit(solution)/shard_map/reduce_scatter | solution.py:1256
  996.7 66.9 %reduce-scatter.30.cloned.1.call-done = f32[1,1,32,1024]{3,2,1,0:T(8,128)} async-done(((f32[8,1,32,1024]{3,2,1,0:T(8,128)}), f32[1,1,32,1024]{3,2,1,0:T(8,128)}) %reduce-scatter.30.cloned.1.call-update) | async-done | bytes 131088 | tf_op jit(solution)/shard_map/reduce_scatter | solution.py:1258
  1063.6 66.4 %reduce-scatter.32.cloned.1.call-done = f32[1,1,32,1024]{3,2,1,0:T(8,128)} async-done(((f32[8,1,32,1024]{3,2,1,0:T(8,128)}), f32[1,1,32,1024]{3,2,1,0:T(8,128)}) %reduce-scatter.32.cloned.1.call-update) | async-done | bytes 131088 | tf_op jit(solution)/shard_map/reduce_scatter | solution.py:1260
  1130.0 71.1 %reduce-scatter.34.cloned.1.call-done = f32[1,1,32,2048]{3,2,1,0:T(8,128)} async-done(((f32[8,1,32,2048]{3,2,1,0:T(8,128)}), f32[1,1,32,2048]{3,2,1,0:T(8,128)}) %reduce-scatter.34.cloned.1.call-update) | async-done | bytes 262160 | tf_op jit(solution)/shard_map/reduce_scatter | solution.py:1262
  1201.1 71.1 %reduce-scatter.36.cloned.1.call-done = f32[1,1,64,1024]{3,2,1,0:T(8,128)} async-done(((f32[8,1,64,1024]{3,2,1,0:T(8,128)}), f32[1,1,64,1024]{3,2,1,0:T(8,128)}) %reduce-scatter.36.cloned.1.call-update) | async-done | bytes 262160 | tf_op jit(solution)/shard_map/reduce_scatter | solution.py:1264
  (399 shorter events, 287.1 us)
Async XLA Ops:
  7.2 69.2 %copy-start.57 = (bf16[192]{0:T(256)(128)(2,1)S(1)}, bf16[192]{0:T(256)(128)(2,1)}, u32[]{:S(2)}) copy-start(bf16[192]{0:T(256)(128)(2,1)} %param.37) | copy-start | bytes 1156
  7.2 69.2 %copy-start.59 = (bf16[64]{0:T(256)(128)(2,1)S(1)}, bf16[64]{0:T(256)(128)(2,1)}, u32[]{:S(2)}) copy-start(bf16[64]{0:T(256)(128)(2,1)} %param.33) | copy-start | bytes 388
  7.2 69.2 %copy-start.58 = (bf16[32]{0:T(256)(128)(2,1)S(1)}, bf16[32]{0:T(256)(128)(2,1)}, u32[]{:S(2)}) copy-start(bf16[32]{0:T(256)(128)(2,1)} %param.35) | copy-start | bytes 196
  7.2 69.2 %copy-start.61 = (bf16[32]{0:T(256)(128)(2,1)S(1)}, bf16[32]{0:T(256)(128)(2,1)}, u32[]{:S(2)}) copy-start(bf16[32]{0:T(256)(128)(2,1)} %param.29) | copy-start | bytes 196
  7.2 69.2 %copy-start.60 = (bf16[32]{0:T(256)(128)(2,1)S(1)}, bf16[32]{0:T(256)(128)(2,1)}, u32[]{:S(2)}) copy-start(bf16[32]{0:T(256)(128)(2,1)} %param.31) | copy-start | bytes 196
  7.2 69.3 %copy-start.63 = (bf16[32]{0:T(256)(128)(2,1)S(1)}, bf16[32]{0:T(256)(128)(2,1)}, u32[]{:S(2)}) copy-start(bf16[32]{0:T(256)(128)(2,1)} %param.25) | copy-start | bytes 196
  7.2 69.3 %copy-start.62 = (bf16[32]{0:T(256)(128)(2,1)S(1)}, bf16[32]{0:T(256)(128)(2,1)}, u32[]{:S(2)}) copy-start(bf16[32]{0:T(256)(128)(2,1)} %param.27) | copy-start | bytes 196
  7.3 515.4 %all-gather.10.cloned.1.call-start = ((), (), s32[]{:S(2)}) async-start(), calls=%async_computation.12 | async-start | bytes 2621440 | tf_op jit(solution)/shard_map/all_gather | solution.py:1025
  42.8 484.0 %all-gather.8.cloned.1.call-start = ((), (), s32[]{:S(2)}) async-start(), calls=%async_computation.11 | async-start | bytes 2621440 | tf_op jit(solution)/shard_map/all_gather | solution.py:1025
  77.2 130.7 %copy-start.64 = (s32[1,4]{1,0:T(1,128)S(1)}, s32[1,4]{1,0:T(1,128)}, u32[]{:S(2)}) copy-start(s32[1,4]{1,0:T(1,128)} %lens.1) | copy-start | bytes 52
  208.2 97.1 %copy-start.40 = (s32[384]{0:T(512)}, s32[384]{0:T(512)S(1)}, u32[]{:S(2)}) copy-start(s32[384]{0:T(512)S(1)} %broadcast_add_fusion.1) | copy-start | bytes 4612
  259.0 50.9 %all-to-all-start = ((bf16[4,2,49152]{2,1,0:T(2,128)(2,1)}), bf16[4,2,49152]{2,1,0:T(2,128)(2,1)}, u32[]{:S(2)}, u32[]{:S(2)}) async-start(bf16[4,2,49152]{2,1,0:T(2,128)(2,1)} %reshape.926), calls=%async_computation | async-start | bytes 1572864 | tf_op jit(solution)/shard_map/all_to_all | solution.py:1094
  263.2 267.4 %all-gather.12.cloned.1.call-start = ((), (), s32[]{:S(2)}) async-start(), calls=%async_computation.13 | async-start | bytes 2621440 | tf_op jit(solution)/shard_map/all_gather | solution.py:1025
  448.7 30.3 %all-to-all-start.2 = ((bf16[4,2,49152]{2,1,0:T(2,128)(2,1)}), bf16[4,2,49152]{2,1,0:T(2,128)(2,1)S(1)}, u32[]{:S(2)}, u32[]{:S(2)}) async-start(bf16[4,2,49152]{2,1,0:T(2,128)(2,1)} %reshape.930), calls=%async_computation.2 | async-start | bytes 1572864 | tf_op jit(solution)/shard_map/all_to_all | solution.py:1153
  478.9 20.5 %all-to-all-start.1 = ((bf16[4,2,49152]{2,1,0:T(2,128)(2,1)}), bf16[4,2,49152]{2,1,0:T(2,128)(2,1)}, u32[]{:S(2)}, u32[]{:S(2)}) async-start(bf16[4,2,49152]{2,1,0:T(2,128)(2,1)} %reshape.928), calls=%async_computation.1 | async-start | bytes 1572864 | tf_op jit(solution)/shard_map/all_to_all | solution.py:1150
  499.4 15.9 %all-to-all-start.3 = ((bf16[4,2,49152]{2,1,0:T(2,128)(2,1)}), bf16[4,2,49152]{2,1,0:T(2,128)(2,1)}, u32[]{:S(2)}, u32[]{:S(2)}) async-start(bf16[4,2,49152]{2,1,0:T(2,128)(2,1)} %reshape.932), calls=%async_computation.3 | async-start | bytes 1572864 | tf_op jit(solution)/shard_map/all_to_all | solution.py:1160
  503.6 336.7 %all-reduce.35.cloned.1.call-start = ((), (), s32[]{:S(2)}) async-start(), calls=%async_computation.21 | async-start | bytes 33554432
  549.0 380.4 %reduce-scatter.38.cloned.1.call-start = ((), (), s32[]{:S(2)}) async-start(), calls=%async_computation.20 | async-start | bytes 20480 | tf_op jit(solution)/shard_map/reduce_scatter | solution.py:1249
  567.6 403.3 %reduce-scatter.26.cloned.1.call-start = ((), (), s32[]{:S(2)}) async-start(), calls=%async_computation.14 | async-start | bytes 1179648 | tf_op jit(solution)/shard_map/reduce_scatter | solution.py:1254
  843.2 153.5 %reduce-scatter.28.cloned.1.call-start = ((), (), s32[]{:S(2)}) async-start(), calls=%async_computation.15 | async-start | bytes 1179648 | tf_op jit(solution)/shard_map/reduce_scatter | solution.py:1256
  846.1 217.5 %reduce-scatter.30.cloned.1.call-start = ((), (), s32[]{:S(2)}) async-start(), calls=%async_computation.16 | async-start | bytes 1179648 | tf_op jit(solution)/shard_map/reduce_scatter | solution.py:1258
  848.9 281.1 %reduce-scatter.32.cloned.1.call-start = ((), (), s32[]{:S(2)}) async-start(), calls=%async_computation.17 | async-start | bytes 1179648 | tf_op jit(solution)/shard_map/reduce_scatter | solution.py:1260
  851.9 349.3 %reduce-scatter.34.cloned.1.call-start = ((), (), s32[]{:S(2)}) async-start(), calls=%async_computation.18 | async-start | bytes 2359296 | tf_op jit(solution)/shard_map/reduce_scatter | solution.py:1262
  855.4 416.8 %reduce-scatter.36.cloned.1.call-start = ((), (), s32[]{:S(2)}) async-start(), calls=%async_computation.19 | async-start | bytes 2359296 | tf_op jit(solution)/shard_map/reduce_scatter | solution.py:1264
  (83 other events, 509.9 us)
Sparse Core Ops, SparseCore 0:
  42.9 23.6 all-gather.9
  76.5 35.1 all-gather.7
  298.5 24.2 all-gather.11
  549.1 291.1 all-reduce.34
  842.6 19.2 reduce-scatter.37
  866.1 63.7 reduce-scatter.25
  933.9 62.7 reduce-scatter.27
  1001.1 62.4 reduce-scatter.29
  1067.6 62.3 reduce-scatter.31
  1134.4 66.7 reduce-scatter.33
  1205.7 66.5 reduce-scatter.35
